TPU v7x, 32 devices: a whole 2x2x4 slice. The times are simulated.
32 devices in a mesh: dp: 8 (over z, x), section: 4 (over y, core).
Axes of the slice: x: 2, y: 2, z: 4, core: 2. Of those that a mesh axis runs over, the one named last changes fastest.
Arguments:
- tokens: bfloat16 [16384, 768], P(('dp', 'section')), may hold values from -6 to 6
- cotangent: bfloat16 [16384, 768], P(('dp', 'section')), may hold values from -6 to 6
- doc_ids: int32 [16, 1024], P('dp'), may hold values from 0 to 7, never falling along the last dimension, each value on 1 to 512 neighbouring positions
- gain_attn: float32 [4, 768], P('section'), may hold values from 0.5 to 1.5
- w_qkv: bfloat16 [4, 768, 2304], P('section'), may hold values from -0.21875 to 0.21875
- w_out: bfloat16 [4, 768, 768], P('section'), may hold values from -1.75 to 1.75
- gain_mlp: float32 [4, 768], P('section'), may hold values from 0.5 to 1.5
- w_up: bfloat16 [4, 768, 3072], P('section'), may hold values from -0.21875 to 0.21875
- w_down: bfloat16 [4, 3072, 768], P('section'), may hold values from -0.109375 to 0.109375
Outputs:
- output: bfloat16 [16384, 768], P(('dp', 'section'))
- input_grad: bfloat16 [16384, 768], P(('dp', 'section'))
- grad_gain_attn: float32 [4, 768], P('section', 'dp')
- grad_qkv: float32 [4, 768, 2304], P('section', 'dp')
- grad_out: float32 [4, 768, 768], P('section', 'dp')
- grad_gain_mlp: float32 [4, 768], P('section', 'dp')
- grad_up: float32 [4, 768, 3072], P('section', 'dp')
- grad_down: float32 [4, 3072, 768], P('section', 'dp')
Inputs may be any that keep to these rules, and one draw needn't show every extreme that they name: `doc_ids`: along each packed row of 1024 tokens the numbers never fall; each of the 8 documents of a row has 1 to 512 tokens, and one has exactly 512.
All inputs are finite; a program needn't handle non-finite values.
Results may differ from a plain program's by a relative error of at most 0.025.
Values may be sent and summed in bfloat16 or wider, within the bound.
A program may use at most 512 MiB of HBM per device.

v0:
```python
from functools import partial

import jax
import jax.numpy as jnp
from jax import lax
from jax.sharding import PartitionSpec as P

D = 768
HEADS = 12
HD = 64
FF = 3072


epsilon = 1e-05
neg_big = -1e30


def passed_along(block, axis, distance):
    devices = range(lax.axis_size(axis))
    route = [(i - distance, i) for i in devices if i - distance in devices]
    return lax.ppermute(block, axis, route)


def scaled_norm(values, gain_vec):
    factor = lax.rsqrt(jnp.mean(values * values, axis=-1, keepdims=True) + epsilon)
    return values * factor * gain_vec


def center_rows(values):
    return values - jnp.mean(values, axis=-1, keepdims=True)


def matmul(left_side, right_side):
    return jnp.dot(left_side, right_side, preferred_element_type=jnp.float32)


def matmul_rt(left_side, right_side):
    return lax.dot_general(
        left_side, right_side, (((1,), (1,)), ((), ())), preferred_element_type=jnp.float32
    )


def matmul_lt(left_side, right_side):
    return lax.dot_general(
        left_side, right_side, (((0,), (0,)), ((), ())), preferred_element_type=jnp.float32
    )


def split_heads(triple):
    seq_len = triple.shape[0]
    width = triple.shape[1] // 3
    shaped = triple.reshape(seq_len, 3, width // HD, HD)
    return (shaped[:, 0], shaped[:, 1], shaped[:, 2])


def block_layout(seq_len):
    block_rows = min(512, seq_len)
    return (block_rows, seq_len // block_rows)


def block_scores(query_part, keys_all, doc_ids, first_row):
    block_rows = query_part.shape[0]
    seq_len = keys_all.shape[0]
    scores = jnp.einsum(
        "qhd,khd->hqk", query_part, keys_all, preferred_element_type=jnp.float32
    ) * HD ** (-0.5)
    rows_at = first_row + jnp.arange(block_rows, dtype=jnp.int32)
    cols_at = jnp.arange(seq_len, dtype=jnp.int32)
    row_docs = lax.dynamic_slice_in_dim(doc_ids, first_row, block_rows)
    allowed = (cols_at[None, :] <= rows_at[:, None]) & (row_docs[:, None] == doc_ids[None, :])
    return jnp.where(allowed[None], scores, neg_big)


def attend_forward(triple, doc_ids):
    queries, keys_all, values_all = split_heads(triple)
    seq_len = triple.shape[0]
    block_rows, blocks = block_layout(seq_len)
    query_blocks = queries.reshape(blocks, block_rows, queries.shape[1], HD)
    starts = jnp.arange(blocks, dtype=jnp.int32) * block_rows

    def one_block(packed):
        query_part, first_row = packed
        scores = block_scores(query_part, keys_all, doc_ids, first_row)
        row_max = jnp.max(scores, axis=-1, keepdims=True)
        powered = jnp.exp(scores - row_max)
        row_total = jnp.sum(powered, axis=-1, keepdims=True)
        attn_probs = (powered / row_total).astype(jnp.bfloat16)
        mixed_heads = jnp.einsum(
            "hqk,khd->qhd", attn_probs, values_all, preferred_element_type=jnp.float32
        )
        return (mixed_heads.astype(jnp.bfloat16), (row_max + jnp.log(row_total))[..., 0])

    mixed_heads, log_totals = lax.map(one_block, (query_blocks, starts))
    return (mixed_heads.reshape(seq_len, -1), log_totals)


def attend_backward(triple, doc_ids, log_totals, grad_mixed):
    queries, keys_all, values_all = split_heads(triple)
    seq_len = triple.shape[0]
    block_rows, blocks = block_layout(seq_len)
    head_count = queries.shape[1]
    query_blocks = queries.reshape(blocks, block_rows, head_count, HD)
    grad_blocks = grad_mixed.reshape(blocks, block_rows, head_count, HD)
    starts = jnp.arange(blocks, dtype=jnp.int32) * block_rows
    scaling = HD ** (-0.5)

    def one_block(carried, packed):
        grad_keys, grad_values = carried
        query_part, grad_part, log_part, first_row = packed
        scores = block_scores(query_part, keys_all, doc_ids, first_row)
        attn_probs = jnp.exp(scores - log_part[..., None])
        grad_probs = jnp.einsum(
            "qhd,khd->hqk", grad_part, values_all, preferred_element_type=jnp.float32
        )
        inner_sum = jnp.sum(attn_probs * grad_probs, axis=-1, keepdims=True)
        grad_scores = (attn_probs * (grad_probs - inner_sum)).astype(jnp.bfloat16)
        grad_query = (
            jnp.einsum("hqk,khd->qhd", grad_scores, keys_all, preferred_element_type=jnp.float32)
            * scaling
        )
        grad_keys = (
            grad_keys
            + jnp.einsum(
                "hqk,qhd->khd", grad_scores, query_part, preferred_element_type=jnp.float32
            )
            * scaling
        )
        grad_values = grad_values + jnp.einsum(
            "hqk,qhd->khd",
            attn_probs.astype(jnp.bfloat16),
            grad_part,
            preferred_element_type=jnp.float32,
        )
        return ((grad_keys, grad_values), grad_query)

    zero_keys = jnp.zeros(keys_all.shape, jnp.float32)
    (grad_keys, grad_values), grad_queries = lax.scan(
        one_block, (zero_keys, zero_keys), (query_blocks, grad_blocks, log_totals, starts)
    )
    joined = jnp.concatenate(
        [
            grad_queries.reshape(seq_len, -1),
            grad_keys.reshape(seq_len, -1),
            grad_values.reshape(seq_len, -1),
        ],
        axis=1,
    )
    return joined.astype(jnp.bfloat16)


def layer_forward(stream, doc_ids, params):
    gain_a, weight_qkv, weight_o, gain_m, weight_up, weight_down = params
    normed_attn = scaled_norm(stream, gain_a).astype(jnp.bfloat16)
    triple = matmul(normed_attn, weight_qkv).astype(jnp.bfloat16)
    mixed_heads, log_totals = attend_forward(triple, doc_ids)
    branch = matmul(mixed_heads, weight_o)
    middle = stream + center_rows(branch)
    normed_mlp = scaled_norm(middle, gain_m).astype(jnp.bfloat16)
    hidden = matmul(normed_mlp, weight_up)
    active = jax.nn.gelu(hidden, approximate=True).astype(jnp.bfloat16)
    branch = matmul(active, weight_down)
    result = middle + center_rows(branch)
    return (
        result,
        (stream, normed_attn, triple, mixed_heads, log_totals, middle, normed_mlp, hidden, active),
    )


def layer_backward(grad_result, doc_ids, params, kept_acts):
    gain_a, weight_qkv, weight_o, gain_m, weight_up, weight_down = params
    stream, normed_attn, triple, mixed_heads, log_totals, middle, normed_mlp, hidden, active = (
        kept_acts
    )
    grad_branch = center_rows(grad_result).astype(jnp.bfloat16)
    grad_down = matmul_lt(active, grad_branch)
    grad_active = matmul_rt(grad_branch, weight_down)
    _, gelu_pull = jax.vjp(partial(jax.nn.gelu, approximate=True), hidden)
    grad_hidden = gelu_pull(grad_active)[0].astype(jnp.bfloat16)
    grad_up = matmul_lt(normed_mlp, grad_hidden)
    grad_normed = matmul_rt(grad_hidden, weight_up)
    _, norm_pull = jax.vjp(scaled_norm, middle, gain_m)
    grad_middle, grad_gain_m = norm_pull(grad_normed)
    grad_middle = grad_middle + grad_result
    grad_branch = center_rows(grad_middle).astype(jnp.bfloat16)
    grad_o = matmul_lt(mixed_heads, grad_branch)
    grad_mixed = matmul_rt(grad_branch, weight_o).astype(jnp.bfloat16)
    grad_triple = attend_backward(triple, doc_ids, log_totals, grad_mixed)
    grad_qkv = matmul_lt(normed_attn, grad_triple)
    grad_normed = matmul_rt(grad_triple, weight_qkv)
    _, norm_pull = jax.vjp(scaled_norm, stream, gain_a)
    grad_stream, grad_gain_a = norm_pull(grad_normed)
    return (
        grad_stream + grad_middle,
        (grad_gain_a, grad_qkv, grad_o, grad_gain_m, grad_up, grad_down),
    )


def body(tokens, cotangent, doc_ids, gain_attn, w_qkv, w_out, gain_mlp, w_up, w_down):
    sections = lax.axis_size("section")
    section_index = lax.axis_index("section")
    micro_count, seq_len = doc_ids.shape
    block_rows, blocks = block_layout(seq_len)
    params = (gain_attn[0], w_qkv[0], w_out[0], gain_mlp[0], w_up[0], w_down[0])
    whole_tokens, whole_cot = (
        lax.all_gather(tokens, "section", axis=0, tiled=True),
        lax.all_gather(cotangent, "section", axis=0, tiled=True),
    )
    centered = center_rows(whole_tokens.astype(jnp.float32)).reshape(micro_count, seq_len, D)
    cot_rows = whole_cot.astype(jnp.float32).reshape(micro_count, seq_len, D)
    ticks = micro_count + sections - 1
    kept_init = (
        jnp.zeros((micro_count, seq_len, D), jnp.float32),
        jnp.zeros((micro_count, seq_len, D), jnp.bfloat16),
        jnp.zeros((micro_count, seq_len, 3 * D), jnp.bfloat16),
        jnp.zeros((micro_count, seq_len, D), jnp.bfloat16),
        jnp.zeros((micro_count, blocks, HEADS, block_rows), jnp.float32),
        jnp.zeros((micro_count, seq_len, D), jnp.float32),
        jnp.zeros((micro_count, seq_len, D), jnp.bfloat16),
        jnp.zeros((micro_count, seq_len, FF), jnp.float32),
        jnp.zeros((micro_count, seq_len, FF), jnp.bfloat16),
    )
    finals_init = jnp.zeros((micro_count, seq_len, D), jnp.float32)
    incoming_init = jnp.zeros((seq_len, D), jnp.bfloat16)

    def forward_tick(tick_index, carried):
        incoming, kept_all, finals = carried
        micro_index = tick_index - section_index
        active_tick = (micro_index >= 0) & (micro_index < micro_count)
        micro_slot = jnp.clip(micro_index, 0, micro_count - 1)
        first_input = lax.dynamic_index_in_dim(centered, micro_slot, 0, keepdims=False)
        stream = jnp.where(section_index == 0, first_input, incoming.astype(jnp.float32))
        row_docs = lax.dynamic_index_in_dim(doc_ids, micro_slot, 0, keepdims=False)

        def forward_compute(buffers):
            kept_now, finals_now = buffers
            result, kept_acts = layer_forward(stream, row_docs, params)
            kept_now = jax.tree.map(
                lambda stacked, single: lax.dynamic_update_index_in_dim(
                    stacked, single, micro_slot, 0
                ),
                kept_now,
                kept_acts,
            )
            finals_now = lax.dynamic_update_index_in_dim(finals_now, result, micro_slot, 0)
            return (result.astype(jnp.bfloat16), kept_now, finals_now)

        def forward_pass_on(buffers):
            return (jnp.zeros_like(incoming), buffers[0], buffers[1])

        sending, kept_all, finals = lax.cond(
            active_tick, forward_compute, forward_pass_on, (kept_all, finals)
        )
        incoming = passed_along(sending, "section", 1)
        return (incoming, kept_all, finals)

    _, kept_all, finals = lax.fori_loop(
        0, ticks, forward_tick, (incoming_init, kept_init, finals_init)
    )
    full_shapes = ((D,), (D, 3 * D), (D, D), (D,), (D, FF), (FF, D))
    zero_full = tuple((jnp.zeros(shape_full, jnp.float32) for shape_full in full_shapes))
    input_init = jnp.zeros((micro_count, seq_len, D), jnp.float32)

    def backward_tick(tick_index, carried):
        incoming, grads_kept, input_grads = carried
        micro_index = tick_index - (sections - 1 - section_index)
        active_tick = (micro_index >= 0) & (micro_index < micro_count)
        micro_slot = jnp.clip(micro_index, 0, micro_count - 1)
        top_grad = lax.dynamic_index_in_dim(cot_rows, micro_slot, 0, keepdims=False)
        grad_result = jnp.where(
            section_index == sections - 1, top_grad, incoming.astype(jnp.float32)
        )
        row_docs = lax.dynamic_index_in_dim(doc_ids, micro_slot, 0, keepdims=False)
        kept_acts = jax.tree.map(
            lambda stacked: lax.dynamic_index_in_dim(stacked, micro_slot, 0, keepdims=False),
            kept_all,
        )

        def backward_compute(input_now):
            grad_stream, layer_grads = layer_backward(grad_result, row_docs, params, kept_acts)
            input_now = lax.dynamic_update_index_in_dim(
                input_now, center_rows(grad_stream), micro_slot, 0
            )
            return (grad_stream.astype(jnp.bfloat16), layer_grads, input_now)

        def backward_pass_on(input_now):
            return (jnp.zeros_like(incoming), zero_full, input_now)

        sending, layer_grads, input_grads = lax.cond(
            active_tick, backward_compute, backward_pass_on, input_grads
        )
        grads_kept = jax.tree.map(lambda older, newer: older + newer, grads_kept, layer_grads)
        incoming = passed_along(sending, "section", -1)
        return (incoming, grads_kept, input_grads)

    _, grads_kept, input_grads = lax.fori_loop(
        0, ticks, backward_tick, (incoming_init, zero_full, input_init)
    )
    shards = lax.psum_scatter(grads_kept, "dp", scatter_dimension=0, tiled=True)
    flat_out = finals.reshape(micro_count * seq_len, D)
    flat_grad = input_grads.reshape(micro_count * seq_len, D)
    out_term = jnp.where(section_index == sections - 1, flat_out, 0.0)
    grad_term = jnp.where(section_index == 0, flat_grad, 0.0)
    out_part, grad_part = (
        lax.psum_scatter(
            out_term.astype(jnp.bfloat16), "section", scatter_dimension=0, tiled=True
        ).astype(jnp.float32),
        lax.psum_scatter(
            grad_term.astype(jnp.bfloat16), "section", scatter_dimension=0, tiled=True
        ).astype(jnp.float32),
    )
    output = out_part.astype(jnp.bfloat16)
    input_grad = grad_part.astype(jnp.bfloat16)
    return (
        output,
        input_grad,
        shards[0][None],
        shards[1][None],
        shards[2][None],
        shards[3][None],
        shards[4][None],
        shards[5][None],
    )


def solution(mesh):
    in_specs = (
        P(("dp", "section"), None),
        P(("dp", "section"), None),
        P("dp", None),
        P("section", None),
        P("section", None, None),
        P("section", None, None),
        P("section", None),
        P("section", None, None),
        P("section", None, None),
    )
    out_specs = (
        P(("dp", "section"), None),
        P(("dp", "section"), None),
        P("section", "dp"),
        P("section", "dp", None),
        P("section", "dp", None),
        P("section", "dp"),
        P("section", "dp", None),
        P("section", "dp", None),
    )
    return jax.shard_map(body, mesh=mesh, in_specs=in_specs, out_specs=out_specs, check_vma=False)
```

profile of v0, /device:TPU:0, one launch (start us, length us, event | category | flops | bytes accessed | tf_op | source)
XLA Modules:
  0.0 3228.0 jit_solution(16148130129760061026)
XLA Ops:
  12.6 28.3 all-gather.3.cloned.1.call-done
  89.7 775.5 %while.112 = (s32[]{:T(128)}, bf16[1024,768]{0,1:T(8,128)(2,1)S(1)}, f32[2,1024,768]{1,2,0:T(8,128)}, bf16[2,1024,768]{1,2,0:T(8,128)(2,1)}, bf16[2,1024,2304]{2...) while((s32[]{:T(128)}, bf16[1024,768]{0,1:T(8,128)(2,1)S(1)}, ...), condition=%wide.region_12.13_spmd, body=%wide.region_1.12_spmd.sunk | while | flops 16264589312 | bytes 676554688 | solution.py:256
  109.6 170.2 %conditional.5 = (bf16[1024,768]{0,1:T(8,128)(2,1)}, f32[2,1024,768]{1,2,0:T(8,128)}, bf16[2,1024,768]{1,2,0:T(8,128)(2,1)}, bf16[2,1024,2304]{2,1,0:T(8,128)(2,...) conditional(s32[]{:T(128)} %convert_element_type.204, ...), branch_computations={%region_2.2_spmd, %region_3.11_spmd} | conditional | flops 16264589312 | bytes 670262656 | solution.py:250
  145.1 76.6 %while.110 = (s32[]{:T(128)}, bf16[2,512,12,64]{1,3,2,0:T(8,128)(2,1)}, f32[2,12,512]{2,1,0:T(8,128)S(1)}, s32[2]{0:T(128)S(1)}, s32[1024]{0:T(1024)S(1)}, /*ind...) while((s32[]{:T(128)}, ...), condition=%wide.region_8.7_spmd, body=%wide.region_5.6_spmd.sunk | while | flops 1688070656 | bytes 189503728 | solution.py:93
  284.4 170.2 %conditional.5 = (bf16[1024,768]{0,1:T(8,128)(2,1)}, f32[2,1024,768]{1,2,0:T(8,128)}, bf16[2,1024,768]{1,2,0:T(8,128)(2,1)}, bf16[2,1024,2304]{2,1,0:T(8,128)(2,...) conditional(s32[]{:T(128)} %convert_element_type.204, ...), branch_computations={%region_2.2_spmd, %region_3.11_spmd} | conditional | flops 16264589312 | bytes 670262656 | solution.py:250
  319.8 76.6 %while.110 = (s32[]{:T(128)}, bf16[2,512,12,64]{1,3,2,0:T(8,128)(2,1)}, f32[2,12,512]{2,1,0:T(8,128)S(1)}, s32[2]{0:T(128)S(1)}, s32[1024]{0:T(1024)S(1)}, /*ind...) while((s32[]{:T(128)}, ...), condition=%wide.region_8.7_spmd, body=%wide.region_5.6_spmd.sunk | while | flops 1688070656 | bytes 189503728 | solution.py:93
  461.4 185.4 %collective-permute-start.1 = (bf16[1024,768]{0,1:T(8,128)(2,1)}, bf16[1024,768]{0,1:T(8,128)(2,1)S(1)}, u32[]{:S(2)}, u32[]{:S(2)}) collective-permute-start(bf16[1024,768]{0,1:T(8,128)(2,1)} %get-tuple-element.2541), channel_id=1, source_target_pairs={{0,1},{1,2},{2,3},{4,5},{5,6},{6,7},{8,9},{9,10},{10,11},{12,13},{... | collective-permute-start | bytes 4718600 | tf_op jit(solution)/shard_map/while/body/eval_jaxpr/ppermute | solution.py:21
  651.2 18.7 collective-permute-start.1
  674.4 187.7 %collective-permute-start.1 = (bf16[1024,768]{0,1:T(8,128)(2,1)}, bf16[1024,768]{0,1:T(8,128)(2,1)S(1)}, u32[]{:S(2)}, u32[]{:S(2)}) collective-permute-start(bf16[1024,768]{0,1:T(8,128)(2,1)} %get-tuple-element.2541), channel_id=1, source_target_pairs={{0,1},{1,2},{2,3},{4,5},{5,6},{6,7},{8,9},{9,10},{10,11},{12,13},{... | collective-permute-start | bytes 4718600 | tf_op jit(solution)/shard_map/while/body/eval_jaxpr/ppermute | solution.py:21
  894.3 1708.0 %while.113 = (s32[]{:T(128)}, bf16[1024,768]{0,1:T(8,128)(2,1)S(1)}, f32[768]{0:T(1024)}, f32[768,2304]{1,0:T(8,128)}, f32[768,768]{1,0:T(8,128)}, /*index=5*/f3...) while((s32[]{:T(128)}, bf16[1024,768]{0,1:T(8,128)(2,1)S(1)}, ...), condition=%wide.region_29.30_spmd.clone, body=%wide.region_14.29_spmd.clone.sunk | while | flops 33260969984 | bytes 824348160 | solution.py:295
  894.7 20.2 conditional.6
  998.0 114.2 %collective-permute-done = bf16[1024,768]{0,1:T(8,128)(2,1)S(1)} collective-permute-done((bf16[1024,768]{0,1:T(8,128)(2,1)}, bf16[1024,768]{0,1:T(8,128)(2,1)S(1)}, u32[]{:S(2)}, u32[]{:S(2)}) %collective-permute-start) | collective-permute-done | bytes 1572896 | tf_op jit(solution)/shard_map/while/body/eval_jaxpr/ppermute | solution.py:21
  1165.3 781.5 %collective-permute-done = bf16[1024,768]{0,1:T(8,128)(2,1)S(1)} collective-permute-done((bf16[1024,768]{0,1:T(8,128)(2,1)}, bf16[1024,768]{0,1:T(8,128)(2,1)S(1)}, u32[]{:S(2)}, u32[]{:S(2)}) %collective-permute-start) | collective-permute-done | bytes 1572896 | tf_op jit(solution)/shard_map/while/body/eval_jaxpr/ppermute | solution.py:21
  1946.8 288.4 %conditional.6 = (bf16[1024,768]{0,1:T(8,128)(2,1)}, f32[768]{0:T(1024)S(1)}, f32[768,2304]{1,0:T(8,128)}, f32[768,768]{1,0:T(8,128)}, f32[768]{0:T(1024)}, /*in...) conditional(s32[]{:T(128)} %convert_element_type.205, ...), branch_computations={%region_15.15_spmd, %region_16.28_spmd} | conditional | flops 33246810112 | bytes 704693312 | solution.py:288
  2012.7 178.6 %while.111 = (s32[]{:T(128)}, f32[1024,12,64]{0,2,1:T(8,128)S(1)}, f32[1024,12,64]{0,2,1:T(8,128)}, bf16[2,512,12,64]{1,3,2,0:T(8,128)(2,1)}, bf16[2,512,12,64]{...) while((s32[]{:T(128)}, f32[1024,12,64]{0,2,1:T(8,128)S(1)}, ...), condition=%wide.region_23.22_spmd.clone, body=%wide.region_21.21_spmd.clone.sunk | while | flops 4126796288 | bytes 246610272 | solution.py:137
  2031.2 18.3 multiply_reduce_fusion.4
  2049.5 22.1 multiply_convert_fusion.6
  2120.2 18.3 multiply_reduce_fusion.4
  2138.4 22.1 multiply_convert_fusion.6
  2273.8 288.4 %conditional.6 = (bf16[1024,768]{0,1:T(8,128)(2,1)}, f32[768]{0:T(1024)S(1)}, f32[768,2304]{1,0:T(8,128)}, f32[768,768]{1,0:T(8,128)}, f32[768]{0:T(1024)}, /*in...) conditional(s32[]{:T(128)} %convert_element_type.205, ...), branch_computations={%region_15.15_spmd, %region_16.28_spmd} | conditional | flops 33246810112 | bytes 704693312 | solution.py:288
  2339.9 178.2 %while.111 = (s32[]{:T(128)}, f32[1024,12,64]{0,2,1:T(8,128)S(1)}, f32[1024,12,64]{0,2,1:T(8,128)}, bf16[2,512,12,64]{1,3,2,0:T(8,128)(2,1)}, bf16[2,512,12,64]{...) while((s32[]{:T(128)}, f32[1024,12,64]{0,2,1:T(8,128)S(1)}, ...), condition=%wide.region_23.22_spmd.clone, body=%wide.region_21.21_spmd.clone.sunk | while | flops 4126796288 | bytes 246610272 | solution.py:137
  2358.0 18.3 multiply_reduce_fusion.4
  2376.3 22.1 multiply_convert_fusion.6
  2447.0 18.3 multiply_reduce_fusion.4
  2465.2 22.1 multiply_convert_fusion.6
  2618.5 22.0 all-reduce.2
  2641.1 31.2 reduce-scatter.13.cloned.1.call-done
  2672.4 40.0 %reduce-scatter.7.cloned.1.call-done = bf16[512,768]{1,0:T(8,128)(2,1)} async-done(((bf16[2048,768]{1,0:T(8,128)(2,1)}), bf16[512,768]{1,0:T(8,128)(2,1)}) %reduce-scatter.7.cloned.1.call-update) | async-done | bytes 786448 | tf_op jit(solution)/shard_map/reduce_scatter | solution.py:304
  2712.3 41.1 %reduce-scatter.9.cloned.1.call-done = bf16[512,768]{1,0:T(8,128)(2,1)} async-done(((bf16[2048,768]{1,0:T(8,128)(2,1)}), bf16[512,768]{1,0:T(8,128)(2,1)}) %reduce-scatter.9.cloned.1.call-update) | async-done | bytes 786448 | tf_op jit(solution)/shard_map/reduce_scatter | solution.py:307
  2753.4 133.1 %reduce-scatter.11.cloned.1.call-done = f32[96,2304]{1,0:T(8,128)} async-done(((f32[768,2304]{1,0:T(8,128)}), f32[96,2304]{1,0:T(8,128)}) %reduce-scatter.11.cloned.1.call-update) | async-done | bytes 884752 | tf_op jit(solution)/shard_map/reduce_scatter | solution.py:298
  2886.6 167.1 %reduce-scatter.15.cloned.1.call-done = f32[96,3072]{1,0:T(8,128)} async-done(((f32[768,3072]{1,0:T(8,128)}), f32[96,3072]{1,0:T(8,128)}) %reduce-scatter.15.cloned.1.call-update) | async-done | bytes 1179664 | tf_op jit(solution)/shard_map/reduce_scatter | solution.py:298
  3053.7 167.2 %reduce-scatter.17.cloned.1.call-done = f32[384,768]{1,0:T(8,128)} async-done(((f32[3072,768]{1,0:T(8,128)}), f32[384,768]{1,0:T(8,128)}) %reduce-scatter.17.cloned.1.call-update) | async-done | bytes 1179664 | tf_op jit(solution)/shard_map/reduce_scatter | solution.py:298
  (716 shorter events, 1122.1 us)
Async XLA Ops:
  7.2 33.7 %all-gather.3.cloned.1.call-start = ((), (), s32[]{:S(2)}) async-start(), calls=%async_computation.6 | async-start | bytes 3932160 | tf_op jit(solution)/shard_map/all_gather | solution.py:205
  7.9 870.0 %all-gather.5.cloned.1.call-start = ((), (), s32[]{:S(2)}) async-start(), calls=%async_computation.8 | async-start | bytes 3932160 | tf_op jit(solution)/shard_map/all_gather | solution.py:206
  8.6 2663.7 %reduce-scatter.13.cloned.1.call-start = ((), (), s32[]{:S(2)}) async-start(), calls=%async_computation.11 | async-start | bytes 2654208 | tf_op jit(solution)/shard_map/reduce_scatter | solution.py:298
  148.9 22.9 copy-start.18
  187.2 22.9 copy-start.18
  279.9 4.5 collective-permute-start.1
  323.6 22.9 copy-start.18
  361.9 22.9 copy-start.18
  454.6 5.4 collective-permute-start.1
  461.4 188.5 %collective-permute-start.1 = (bf16[1024,768]{0,1:T(8,128)(2,1)}, bf16[1024,768]{0,1:T(8,128)(2,1)S(1)}, u32[]{:S(2)}, u32[]{:S(2)}) collective-permute-start(bf16[1024,768]{0,1:T(8,128)(2,1)} %get-tuple-element.2541), channel_id=1, source_target_pairs={{0,1},{1,2},{2,3},{4,5},{5,6},{6,7},{8,9},{9,10},{10,11},{12,13},{... | collective-permute-start | bytes 4718600 | tf_op jit(solution)/shard_map/while/body/eval_jaxpr/ppermute | solution.py:21
  651.2 21.8 collective-permute-start.1
  674.4 190.9 %collective-permute-start.1 = (bf16[1024,768]{0,1:T(8,128)(2,1)}, bf16[1024,768]{0,1:T(8,128)(2,1)S(1)}, u32[]{:S(2)}, u32[]{:S(2)}) collective-permute-start(bf16[1024,768]{0,1:T(8,128)(2,1)} %get-tuple-element.2541), channel_id=1, source_target_pairs={{0,1},{1,2},{2,3},{4,5},{5,6},{6,7},{8,9},{9,10},{10,11},{12,13},{... | collective-permute-start | bytes 4718600 | tf_op jit(solution)/shard_map/while/body/eval_jaxpr/ppermute | solution.py:21
  915.5 29.2 collective-permute-start
  961.4 150.8 %collective-permute-start = (bf16[1024,768]{0,1:T(8,128)(2,1)}, bf16[1024,768]{0,1:T(8,128)(2,1)S(1)}, u32[]{:S(2)}, u32[]{:S(2)}) collective-permute-start(bf16[1024,768]{0,1:T(8,128)(2,1)} %get-tuple-element.2580), channel_id=1, source_target_pairs={{1,0},{2,1},{3,2},{5,4},{6,5},{7,6},{9,8},{10,9},{11,10},{13,12},{... | collective-permute-start | bytes 4718600 | tf_op jit(solution)/shard_map/while/body/eval_jaxpr/ppermute | solution.py:21
  986.8 125.4 %copy-start.51 = (f32[1,768]{1,0:T(1,128)S(1)}, f32[1,768]{1,0:T(1,128)}, u32[]{:S(2)}) copy-start(f32[1,768]{1,0:T(1,128)} %get-tuple-element.2955) | copy-start | bytes 9220 | tf_op jit(solution)/shard_map/while
  1128.6 818.1 %collective-permute-start = (bf16[1024,768]{0,1:T(8,128)(2,1)}, bf16[1024,768]{0,1:T(8,128)(2,1)S(1)}, u32[]{:S(2)}, u32[]{:S(2)}) collective-permute-start(bf16[1024,768]{0,1:T(8,128)(2,1)} %get-tuple-element.2580), channel_id=1, source_target_pairs={{1,0},{2,1},{3,2},{5,4},{6,5},{7,6},{9,8},{10,9},{11,10},{13,12},{... | collective-permute-start | bytes 4718600 | tf_op jit(solution)/shard_map/while/body/eval_jaxpr/ppermute | solution.py:21
  1154.0 792.7 %copy-start.51 = (f32[1,768]{1,0:T(1,128)S(1)}, f32[1,768]{1,0:T(1,128)}, u32[]{:S(2)}) copy-start(f32[1,768]{1,0:T(1,128)} %get-tuple-element.2955) | copy-start | bytes 9220 | tf_op jit(solution)/shard_map/while
  1950.2 34.6 %copy-start.41 = (f32[1024]{0:T(1024)}, f32[1024]{0:T(1024)S(1)}, u32[]{:S(2)}) copy-start(f32[1024]{0:T(1024)S(1)} %get-tuple-element.2137) | copy-start | bytes 12292 | tf_op jit(solution)/shard_map/while/body/eval_jaxpr/cond
  1952.6 19.8 slice-start.6
  1952.6 29.5 slice-start.2
  1955.3 26.8 slice-start.3
  2235.8 37.7 %collective-permute-start = (bf16[1024,768]{0,1:T(8,128)(2,1)}, bf16[1024,768]{0,1:T(8,128)(2,1)S(1)}, u32[]{:S(2)}, u32[]{:S(2)}) collective-permute-start(bf16[1024,768]{0,1:T(8,128)(2,1)} %get-tuple-element.2580), channel_id=1, source_target_pairs={{1,0},{2,1},{3,2},{5,4},{6,5},{7,6},{9,8},{10,9},{11,10},{13,12},{... | collective-permute-start | bytes 4718600 | tf_op jit(solution)/shard_map/while/body/eval_jaxpr/ppermute | solution.py:21
  2277.3 34.7 %copy-start.41 = (f32[1024]{0:T(1024)}, f32[1024]{0:T(1024)S(1)}, u32[]{:S(2)}) copy-start(f32[1024]{0:T(1024)S(1)} %get-tuple-element.2137) | copy-start | bytes 12292 | tf_op jit(solution)/shard_map/while/body/eval_jaxpr/cond
  2279.7 19.9 slice-start.6
  2279.7 29.6 slice-start.2
  2282.3 26.9 slice-start.3
  2562.8 36.6 %collective-permute-start = (bf16[1024,768]{0,1:T(8,128)(2,1)}, bf16[1024,768]{0,1:T(8,128)(2,1)S(1)}, u32[]{:S(2)}, u32[]{:S(2)}) collective-permute-start(bf16[1024,768]{0,1:T(8,128)(2,1)} %get-tuple-element.2580), channel_id=1, source_target_pairs={{1,0},{2,1},{3,2},{5,4},{6,5},{7,6},{9,8},{10,9},{11,10},{13,12},{... | collective-permute-start | bytes 4718600 | tf_op jit(solution)/shard_map/while/body/eval_jaxpr/ppermute | solution.py:21
  2602.3 110.0 %reduce-scatter.7.cloned.1.call-start = ((), (), s32[]{:S(2)}) async-start(), calls=%async_computation.7 | async-start | bytes 3932160 | tf_op jit(solution)/shard_map/reduce_scatter | solution.py:304
  2606.1 147.3 %reduce-scatter.9.cloned.1.call-start = ((), (), s32[]{:S(2)}) async-start(), calls=%async_computation.9 | async-start | bytes 3932160 | tf_op jit(solution)/shard_map/reduce_scatter | solution.py:307
  2615.2 271.4 %reduce-scatter.11.cloned.1.call-start = ((), (), s32[]{:S(2)}) async-start(), calls=%async_computation.10 | async-start | bytes 7962624 | tf_op jit(solution)/shard_map/reduce_scatter | solution.py:298
  2615.8 437.9 %reduce-scatter.15.cloned.1.call-start = ((), (), s32[]{:S(2)}) async-start(), calls=%async_computation.12 | async-start | bytes 10616832 | tf_op jit(solution)/shard_map/reduce_scatter | solution.py:298
  2616.5 604.4 %reduce-scatter.17.cloned.1.call-start = ((), (), s32[]{:S(2)}) async-start(), calls=%async_computation.13 | async-start | bytes 10616832 | tf_op jit(solution)/shard_map/reduce_scatter | solution.py:298
  (173 other events, 1213.9 us)
Sparse Core Ops, SparseCore 0:
  9.6 31.2 all-gather.2
  42.4 28.5 all-gather.4
  2602.4 69.9 reduce-scatter.12
  2675.3 36.9 reduce-scatter.6
  2715.5 37.9 reduce-scatter.8
  2757.5 128.9 reduce-scatter.10
  2891.2 162.4 reduce-scatter.14
  3058.3 162.5 reduce-scatter.16
where the time goes:
time: 3240 us; the launch traced here: 3230 us
  waiting for transfers between devices  1520 us (47%)
  matrix products  508 us (16%)
  other arithmetic  411 us (13%)
  starting transfers between devices  402 us (12%)
  local copies, waits for them, and re-layouts  298 us (9%)
  loops' own time  47.4 us (1%)
    ppermute x10, waiting for transfers between devices, passed_along(): return lax.ppermute(block, axis, route)  912 us
    reduce_scatter x4, waiting for transfers between devices, body(): shards = lax.psum_scatter(grads_kept, 'dp', scatter_dimension=0, tiled=True)  499 us
    ppermute x10, starting transfers between devices, passed_along(): return lax.ppermute(block, axis, route)  402 us
    add x25, other arithmetic, backward_tick(): older + newer  162 us
    dot_general x8, matrix products, block_scores(): jnp.einsum('qhd,khd->hqk', query_part, keys_all, preferred_element_type=j...  96 us
    convert_element_type x4, other arithmetic, one_block(): grad_scores = (attn_probs * (grad_probs - inner_sum)).astype(jnp.bfloat16)  88.4 us
    dot_general x4, matrix products, one_block(): jnp.einsum('qhd,khd->hqk', grad_part, values_all, preferred_element_type=...  73 us
    dot_general x8, matrix products, matmul_rt(): lax.dot_general(left_side, right_side, (((1,), (1,)), ((), ())), preferre...  70.9 us
  transfers between devices with their start and end apart: 18, of which 15 were waited for; matrix products, arithmetic and copies ran while one was open for 17% of the time, Pallas kernels for 0%

commit v1 on v0

v1 whole, which is shorter than its diff:
```python
import functools

import jax
import jax.numpy as jnp
from jax import lax
from jax.experimental import pallas as pl
from jax.experimental.pallas import tpu as pltpu
from jax.sharding import PartitionSpec as P

D = 768
HEADS = 12
HD = 64
FF = 3072
C = 256
WIN = 3
PAIRS = HEADS // 2
EPS = 1e-05
NEG = -1e30
MESH = pl.DeviceIdType.MESH
BF16 = jnp.bfloat16
F32 = jnp.float32
VMEM_LIMIT = 60 * 1024 * 1024


def dot(a, b):
    return jnp.dot(a, b, preferred_element_type=F32)


def dot_nt(a, b):
    return lax.dot_general(a, b, (((1,), (1,)), ((), ())), preferred_element_type=F32)


def row_mean(v):
    return jnp.mean(v, axis=-1, keepdims=True)


def greet(section, sections):
    dp = lax.axis_index("dp")
    barrier = pltpu.get_barrier_semaphore()
    for step in range(1, sections):
        other = lax.rem(section + step, sections)
        pl.semaphore_signal(barrier, inc=1, device_id=(dp, other), device_id_type=MESH)
    pl.semaphore_wait(barrier, sections - 1)


def lane_masks():
    lane = lax.broadcasted_iota(jnp.int32, (1, 2 * HD), 1)
    low = (lane < HD).astype(F32)
    return low.astype(BF16), (1.0 - low).astype(BF16), lane < HD


def two_heads(pair, low, high):
    return jnp.concatenate([pair * low, pair * high], axis=0)


def await_arrival(buf, sem):
    pltpu.make_async_copy(buf, buf, sem).wait()


def scatter_rows(section, sections, per, rows, inbox, sems, send_sems, target):
    dp = lax.axis_index("dp")
    for piece in range(per):
        slot = section * per + piece

        @pl.when(section != target)
        def _():
            pltpu.make_async_remote_copy(
                rows.at[piece],
                inbox.at[slot],
                send_sems.at[piece],
                sems.at[slot],
                device_id=(dp, target),
                device_id_type=MESH,
            ).start()

        @pl.when(section == target)
        def _():
            pltpu.make_async_copy(rows.at[piece], inbox.at[slot], sems.at[slot]).start()


def drain_rows(section, sections, per, rows, send_sems, target):
    for piece in range(per):

        @pl.when(section != target)
        def _():
            pltpu.make_async_copy(rows.at[piece], rows.at[piece], send_sems.at[piece]).wait()


def pass_on(section, chunk, per, last, step, outbox, inbox, result, sends, arrivals, landed, kept):
    dp = lax.axis_index("dp")
    owner = chunk // per

    @pl.when(section != last)
    def _():
        pltpu.make_async_remote_copy(
            outbox.at[chunk],
            inbox.at[chunk],
            sends.at[chunk],
            arrivals.at[chunk],
            device_id=(dp, section + step),
            device_id_type=MESH,
        ).start()

    @pl.when((section == last) & (owner != last))
    def _():
        pltpu.make_async_remote_copy(
            outbox.at[chunk],
            result.at[lax.rem(chunk, per)],
            sends.at[chunk],
            landed.at[lax.rem(chunk, per)],
            device_id=(dp, owner),
            device_id_type=MESH,
        ).start()

    @pl.when((section == last) & (owner == last))
    def _():
        pltpu.make_async_copy(
            outbox.at[chunk], result.at[lax.rem(chunk, per)], kept.at[lax.rem(chunk, per)]
        ).start()


def settle(section, chunks, per, last, outbox, result, sends, landed, kept):
    def one(chunk, carry):
        @pl.when((section != last) | (chunk // per != last))
        def _():
            await_arrival(outbox.at[chunk], sends.at[chunk])

        return carry

    lax.fori_loop(0, chunks, one, 0)
    for piece in range(per):

        @pl.when(section != last)
        def _():
            await_arrival(result.at[piece], landed.at[piece])

        @pl.when(section == last)
        def _():
            await_arrival(result.at[piece], kept.at[piece])


def forward_kernel(
    sections,
    tokens,
    doc_q,
    doc_k,
    gain_a,
    gain_m,
    w_qkv,
    w_out,
    w_up,
    w_down,
    result,
    s_x,
    s_q,
    s_k,
    s_v,
    s_na,
    s_mixed,
    s_lse,
    s_mid,
    s_nm,
    s_act,
    s_dg,
    inbox,
    outbox,
    kbuf,
    vbuf,
    bias,
    b_q,
    b_na,
    b_mixed,
    b_lse,
    b_mid,
    b_nm,
    b_act,
    b_dg,
    arrivals,
    sends,
    first_sends,
    landed,
    kept,
    saves,
):
    section = lax.axis_index("section")
    chunks = inbox.shape[0]
    per = tokens.shape[0]
    greet(section, sections)
    scatter_rows(section, sections, per, tokens, inbox, arrivals, first_sends, 0)
    low, high, is_low = lane_masks()
    kbuf[pl.ds(0, 2 * C), :] = jnp.zeros((2 * C, D), BF16)
    vbuf[pl.ds(0, 2 * C), :] = jnp.zeros((2 * C, D), BF16)
    centered = jnp.where(section == 0, 1.0, 0.0).astype(F32)

    def stores(chunk, slot):
        here = pl.ds(pl.multiple_of((chunk + 2) * C, C), C)
        pairs = (
            (inbox.at[chunk], s_x),
            (kbuf.at[here], s_k),
            (vbuf.at[here], s_v),
            (b_q.at[slot], s_q),
            (b_na.at[slot], s_na),
            (b_mixed.at[slot], s_mixed),
            (b_lse.at[slot], s_lse),
            (b_mid.at[slot], s_mid),
            (b_nm.at[slot], s_nm),
            (b_act.at[slot], s_act),
            (b_dg.at[slot], s_dg),
        )
        return [
            pltpu.make_async_copy(src, dst.at[chunk], saves.at[kind, slot])
            for kind, (src, dst) in enumerate(pairs)
        ]

    def one_chunk(chunk, carry):
        slot = lax.rem(chunk, 2)

        @pl.when(chunk >= 2)
        def _():
            for copy in stores(chunk - 2, slot):
                copy.wait()

        todo = stores(chunk, slot)
        await_arrival(inbox.at[chunk], arrivals.at[chunk])
        todo[0].start()
        x = inbox[chunk].astype(F32)
        x = x - centered * row_mean(x)
        na = (x * lax.rsqrt(row_mean(x * x) + EPS) * gain_a[...]).astype(BF16)
        b_na[slot] = na
        todo[4].start()
        b_q[slot] = (dot(na, w_qkv[:, :D]).astype(BF16) * (HD**-0.5)).astype(BF16)
        here = pl.ds(pl.multiple_of((chunk + 2) * C, C), C)
        kbuf[here, :] = dot(na, w_qkv[:, D : 2 * D]).astype(BF16)
        vbuf[here, :] = dot(na, w_qkv[:, 2 * D :]).astype(BF16)
        todo[1].start()
        todo[2].start()
        todo[3].start()
        for part in range(WIN):
            allowed = doc_q[chunk] == doc_k[chunk + part]
            if part == WIN - 1:
                row = lax.broadcasted_iota(jnp.int32, (C, C), 0)
                col = lax.broadcasted_iota(jnp.int32, (C, C), 1)
                allowed = allowed & (col <= row)
            bias[:, part * C : (part + 1) * C] = jnp.where(allowed, 0.0, NEG)
        window = pl.ds(pl.multiple_of(chunk * C, C), WIN * C)
        lane = lax.broadcasted_iota(jnp.int32, (1, 128), 1)
        lse_all = jnp.zeros((C, 128), F32)
        for pair in range(PAIRS):
            lanes = slice(pair * 2 * HD, (pair + 1) * 2 * HD)
            q2 = two_heads(b_q[slot, :, lanes], low, high)
            s = dot_nt(q2, kbuf[window, lanes]).reshape(2, C, WIN * C) + bias[...][None]
            top = jnp.max(s, axis=-1, keepdims=True)
            e = jnp.exp(s - top)
            total = jnp.sum(e, axis=-1, keepdims=True)
            o = dot(e.astype(BF16).reshape(2 * C, WIN * C), vbuf[window, lanes])
            o = o.reshape(2, C, 2 * HD) * (1.0 / total)
            b_mixed[slot, :, lanes] = jnp.where(is_low, o[0], o[1]).astype(BF16)
            lse = top + jnp.log(total)
            lse_all = jnp.where(lane == 2 * pair, lse[0], lse_all)
            lse_all = jnp.where(lane == 2 * pair + 1, lse[1], lse_all)
        b_lse[slot] = jnp.transpose(lse_all)[:16]
        todo[5].start()
        todo[6].start()
        branch = dot(b_mixed[slot], w_out[...])
        mid = x + branch - row_mean(branch)
        b_mid[slot] = mid
        todo[7].start()
        nm = (mid * lax.rsqrt(row_mean(mid * mid) + EPS) * gain_m[...]).astype(BF16)
        b_nm[slot] = nm
        todo[8].start()
        k0 = 0.7978845608028654
        k1 = 0.044715
        for part in range(FF // D):
            cols = slice(part * D, (part + 1) * D)
            h = dot(nm, w_up[:, cols])
            h2 = h * h
            t = jnp.tanh(h * (k0 + (k0 * k1) * h2))
            half = 0.5 + 0.5 * t
            b_act[slot, :, cols] = (h * half).astype(BF16)
            slope = half + (h * (1.0 - t * t)) * (0.5 * k0 + (1.5 * k0 * k1) * h2)
            b_dg[slot, :, cols] = slope.astype(BF16)
        todo[9].start()
        todo[10].start()
        branch = dot(b_act[slot], w_down[...])
        outbox[chunk] = (b_mid[slot] + branch - row_mean(branch)).astype(BF16)
        pass_on(section, chunk, per, sections - 1, 1, outbox, inbox, result, sends, arrivals, landed, kept)
        return carry

    lax.fori_loop(0, chunks, one_chunk, 0)
    for chunk in (chunks - 2, chunks - 1):
        for copy in stores(chunk, chunk % 2):
            copy.wait()
    drain_rows(section, sections, per, tokens, first_sends, 0)
    settle(section, chunks, per, sections - 1, outbox, result, sends, landed, kept)


def backward_kernel(
    sections,
    cotangent,
    doc_qr,
    doc_kc,
    gain_a,
    gain_m,
    w_qkv,
    w_out,
    w_up,
    w_down,
    s_x,
    s_q,
    s_k,
    s_v,
    s_mixed,
    s_lse,
    s_mid,
    s_dg,
    result,
    gains,
    s_db,
    s_dh,
    s_da,
    s_dt,
    inbox,
    outbox,
    kbuf,
    vbuf,
    bias,
    dk_acc,
    dv_acc,
    lse_d,
    marks,
    b_x,
    b_q,
    b_mixed,
    b_lse,
    b_mid,
    b_dg,
    b_db,
    b_dh,
    b_da,
    b_dt,
    arrivals,
    sends,
    first_sends,
    landed,
    kept,
    loads,
    saves,
    kv_sems,
):
    section = lax.axis_index("section")
    chunks = inbox.shape[0]
    per = cotangent.shape[0]
    last = sections - 1

    def fetches(chunk, slot):
        pairs = (
            (s_dg, b_dg),
            (s_mid, b_mid),
            (s_mixed, b_mixed),
            (s_q, b_q),
            (s_lse, b_lse),
            (s_x, b_x),
        )
        return [
            pltpu.make_async_copy(src.at[chunk], dst.at[slot], loads.at[kind, slot])
            for kind, (src, dst) in enumerate(pairs)
        ]

    def stores(chunk, slot):
        pairs = ((b_db, s_db), (b_dh, s_dh), (b_da, s_da), (b_dt, s_dt))
        return [
            pltpu.make_async_copy(src.at[slot], dst.at[chunk], saves.at[kind, slot])
            for kind, (src, dst) in enumerate(pairs)
        ]

    kv_copies = [
        pltpu.make_async_copy(s_k, kbuf.at[pl.ds(2 * C, chunks * C)], kv_sems.at[0]),
        pltpu.make_async_copy(s_v, vbuf.at[pl.ds(2 * C, chunks * C)], kv_sems.at[1]),
    ]
    for copy in fetches(chunks - 1, 0):
        copy.start()
    for copy in kv_copies:
        copy.start()
    greet(section, sections)
    scatter_rows(section, sections, per, cotangent, inbox, arrivals, first_sends, last)
    low, high, _ = lane_masks()
    kbuf[pl.ds(0, 2 * C), :] = jnp.zeros((2 * C, D), BF16)
    vbuf[pl.ds(0, 2 * C), :] = jnp.zeros((2 * C, D), BF16)
    dk_acc[...] = jnp.zeros_like(dk_acc)
    dv_acc[...] = jnp.zeros_like(dv_acc)
    gains[...] = jnp.zeros_like(gains)
    owner_of = lax.broadcasted_iota(jnp.int32, (D, 128), 0) // HD
    marks[...] = (owner_of == lax.broadcasted_iota(jnp.int32, (D, 128), 1)).astype(F32).astype(BF16)
    centered = jnp.where(section == 0, 1.0, 0.0).astype(F32)
    for copy in kv_copies:
        copy.wait()

    def folded(v):
        return jnp.sum(v.reshape(C // 8, 8, D), axis=0)

    def one_chunk(step, carry):
        chunk = chunks - 1 - step
        slot = lax.rem(step, 2)

        @pl.when(step + 1 < chunks)
        def _():
            for copy in fetches(chunk - 1, 1 - slot):
                copy.start()

        @pl.when(step >= 2)
        def _():
            for copy in stores(chunk + 2, slot):
                copy.wait()

        for copy in fetches(chunk, slot):
            copy.wait()
        todo = stores(chunk, slot)
        await_arrival(inbox.at[chunk], arrivals.at[chunk])
        g = inbox[chunk].astype(F32)
        db = (g - row_mean(g)).astype(BF16)
        b_db[slot] = db
        todo[0].start()
        for part in range(FF // D):
            cols = slice(part * D, (part + 1) * D)
            d_active = dot_nt(db, w_down[cols, :])
            b_dh[slot, :, cols] = (d_active * b_dg[slot, :, cols].astype(F32)).astype(BF16)
        todo[1].start()
        dn = dot_nt(b_dh[slot], w_up[...])
        mid = b_mid[slot]
        factor = lax.rsqrt(row_mean(mid * mid) + EPS)
        unit = mid * factor
        gains[1] += folded(dn * unit)
        dn = dn * gain_m[...]
        d_mid = g + factor * (dn - unit * row_mean(dn * unit))
        da = (d_mid - row_mean(d_mid)).astype(BF16)
        b_da[slot] = da
        todo[2].start()
        b_mid[slot] = d_mid
        dmix = dot_nt(da, w_out[...]).astype(BF16)
        prod = dmix.astype(F32) * b_mixed[slot].astype(F32)
        top = prod.astype(BF16)
        rest = (prod - top.astype(F32)).astype(BF16)
        inner = dot(top, marks[...]) + dot(rest, marks[...])
        lse_d[...] = jnp.transpose(inner)[:16]
        for part in range(WIN):
            allowed = doc_kc[chunk + part] == doc_qr[chunk]
            if part == WIN - 1:
                key = lax.broadcasted_iota(jnp.int32, (C, C), 0)
                query = lax.broadcasted_iota(jnp.int32, (C, C), 1)
                allowed = allowed & (key <= query)
            bias[part * C : (part + 1) * C, :] = jnp.where(allowed, 0.0, NEG)
        window = pl.ds(pl.multiple_of(chunk * C, C), WIN * C)
        for pair in range(PAIRS):
            lanes = slice(pair * 2 * HD, (pair + 1) * 2 * HD)
            q2 = two_heads(b_q[slot, :, lanes], low, high)
            do2 = two_heads(dmix[:, lanes], low, high)
            keys = kbuf[window, lanes]
            values = vbuf[window, lanes]
            both = jnp.concatenate([bias[...], bias[...]], axis=1)
            lse = jnp.concatenate(
                [b_lse[slot, 2 * pair : 2 * pair + 1, :], b_lse[slot, 2 * pair + 1 : 2 * pair + 2, :]], axis=1
            )
            inner = jnp.concatenate(
                [lse_d[2 * pair : 2 * pair + 1, :], lse_d[2 * pair + 1 : 2 * pair + 2, :]], axis=1
            )
            probs = jnp.exp(dot_nt(keys, q2) + both - lse)
            ds = (probs * (dot_nt(values, do2) - inner)).astype(BF16)
            dv = dot(probs.astype(BF16), do2)
            dk = dot(ds, q2)
            for part in range(WIN):
                place = lax.rem(chunk + part, WIN)
                rows = slice(part * C, (part + 1) * C)
                dv_acc[place, :, lanes] += dv[rows]
                dk_acc[place, :, lanes] += dk[rows]
            dq = dot(jnp.transpose(keys), ds)
            dq = jnp.concatenate([dq[:HD, :C], dq[HD:, C:]], axis=0)
            b_dt[slot, :, lanes] = (jnp.transpose(dq) * (HD**-0.5)).astype(BF16)
        done = lax.rem(chunk + WIN - 1, WIN)
        b_dt[slot, :, D : 2 * D] = dk_acc[done].astype(BF16)
        b_dt[slot, :, 2 * D :] = dv_acc[done].astype(BF16)
        dk_acc[done] = jnp.zeros((C, D), F32)
        dv_acc[done] = jnp.zeros((C, D), F32)
        todo[3].start()
        dn = dot_nt(b_dt[slot], w_qkv[...])
        x = b_x[slot].astype(F32)
        x = x - centered * row_mean(x)
        factor = lax.rsqrt(row_mean(x * x) + EPS)
        unit = x * factor
        gains[0] += folded(dn * unit)
        dn = dn * gain_a[...]
        grad = b_mid[slot] + factor * (dn - unit * row_mean(dn * unit))
        grad = grad - centered * row_mean(grad)
        outbox[chunk] = grad.astype(BF16)
        pass_on(section, chunk, per, 0, -1, outbox, inbox, result, sends, arrivals, landed, kept)
        return carry

    lax.fori_loop(0, chunks, one_chunk, 0)
    for step in (chunks - 2, chunks - 1):
        for copy in stores(chunks - 1 - step, step % 2):
            copy.wait()
    drain_rows(section, sections, per, cotangent, first_sends, last)
    settle(section, chunks, per, 0, outbox, result, sends, landed, kept)


ANY = pl.BlockSpec(memory_space=pl.ANY)
IN_VMEM = pl.BlockSpec(memory_space=pltpu.VMEM)
DMA = pltpu.SemaphoreType.DMA


def forward(sections, chunks, tokens, doc_q, doc_k, weights):
    per = chunks // sections
    sds = jax.ShapeDtypeStruct
    saved = (
        ("x", (C, D), BF16),
        ("q", (C, D), BF16),
        ("k", (C, D), BF16),
        ("v", (C, D), BF16),
        ("na", (C, D), BF16),
        ("mixed", (C, D), BF16),
        ("lse", (16, C), F32),
        ("mid", (C, D), F32),
        ("nm", (C, D), BF16),
        ("act", (C, FF), BF16),
        ("dg", (C, FF), BF16),
    )
    staged = [entry for entry in saved if entry[0] not in ("x", "k", "v")]
    outs = pl.pallas_call(
        functools.partial(forward_kernel, sections),
        out_shape=[sds((per, C, D), BF16)] + [sds((chunks,) + s, t) for _, s, t in saved],
        in_specs=[ANY] + [IN_VMEM] * 8,
        out_specs=[ANY] * (1 + len(saved)),
        scratch_shapes=[
            pltpu.VMEM((chunks, C, D), BF16),
            pltpu.VMEM((chunks, C, D), BF16),
            pltpu.VMEM(((chunks + 2) * C, D), BF16),
            pltpu.VMEM(((chunks + 2) * C, D), BF16),
            pltpu.VMEM((C, WIN * C), F32),
        ]
        + [pltpu.VMEM((2,) + s, t) for _, s, t in staged]
        + [DMA((chunks,)), DMA((chunks,)), DMA((per,)), DMA((per,)), DMA((per,)), DMA((11, 2))],
        compiler_params=pltpu.CompilerParams(
            collective_id=0, has_side_effects=True, vmem_limit_bytes=VMEM_LIMIT
        ),
        name="layer_forward",
    )(tokens.reshape(per, C, D), doc_q, doc_k, *weights)
    return outs[0], {name: out for (name, _, _), out in zip(saved, outs[1:])}


def backward(sections, chunks, cotangent, doc_qr, doc_kc, weights, kept):
    per = chunks // sections
    sds = jax.ShapeDtypeStruct
    fetched = (
        ((C, D), BF16),
        ((C, D), BF16),
        ((C, D), BF16),
        ((16, C), F32),
        ((C, D), F32),
        ((C, FF), BF16),
    )
    saved = ((C, D), (C, FF), (C, D), (C, 3 * D))
    outs = pl.pallas_call(
        functools.partial(backward_kernel, sections),
        out_shape=[sds((per, C, D), BF16), sds((2, 8, D), F32)] + [sds((chunks,) + s, BF16) for s in saved],
        in_specs=[ANY] + [IN_VMEM] * 8 + [ANY] * 8,
        out_specs=[ANY, IN_VMEM] + [ANY] * len(saved),
        scratch_shapes=[
            pltpu.VMEM((chunks, C, D), BF16),
            pltpu.VMEM((chunks, C, D), BF16),
            pltpu.VMEM(((chunks + 2) * C, D), BF16),
            pltpu.VMEM(((chunks + 2) * C, D), BF16),
            pltpu.VMEM((WIN * C, C), F32),
            pltpu.VMEM((WIN, C, D), F32),
            pltpu.VMEM((WIN, C, D), F32),
            pltpu.VMEM((16, C), F32),
            pltpu.VMEM((D, 128), BF16),
        ]
        + [pltpu.VMEM((2,) + s, t) for s, t in fetched]
        + [pltpu.VMEM((2,) + s, BF16) for s in saved]
        + [DMA((chunks,)), DMA((chunks,)), DMA((per,)), DMA((per,)), DMA((per,))]
        + [DMA((6, 2)), DMA((4, 2)), DMA((2,))],
        compiler_params=pltpu.CompilerParams(
            collective_id=1, has_side_effects=True, vmem_limit_bytes=VMEM_LIMIT
        ),
        name="layer_backward",
    )(
        cotangent.reshape(per, C, D),
        doc_qr,
        doc_kc,
        *weights,
        kept["x"],
        kept["q"],
        kept["k"].reshape(chunks * C, D),
        kept["v"].reshape(chunks * C, D),
        kept["mixed"],
        kept["lse"],
        kept["mid"],
        kept["dg"],
    )
    return outs


def matmul_lt(left_side, right_side):
    rows = left_side.shape[0] * left_side.shape[1]
    return lax.dot_general(
        left_side.reshape(rows, -1),
        right_side.reshape(rows, -1),
        (((0,), (0,)), ((), ())),
        preferred_element_type=F32,
    )


def body(tokens, cotangent, doc_ids, gain_attn, w_qkv, w_out, gain_mlp, w_up, w_down):
    sections = lax.axis_size("section")
    rows, seq = doc_ids.shape
    chunks = rows * seq // C
    docs = doc_ids + 1 + 16 * jnp.arange(rows, dtype=jnp.int32)[:, None]
    docs_q = docs.reshape(chunks, C)
    docs_k = jnp.concatenate([jnp.zeros((2, C), jnp.int32), docs_q])
    weights = (gain_attn, gain_mlp, w_qkv[0], w_out[0], w_up[0], w_down[0])
    output, kept = forward(sections, chunks, tokens, docs_q[:, :, None], docs_k[:, None, :], weights)
    input_grad, gains, db, dh, da, dt = backward(
        sections, chunks, cotangent, docs_q[:, None, :], docs_k[:, :, None], weights, kept
    )
    gains = jnp.sum(gains, axis=1)
    grads = (
        gains[0],
        matmul_lt(kept["na"], dt),
        matmul_lt(kept["mixed"], da),
        gains[1],
        matmul_lt(kept["nm"], dh),
        matmul_lt(kept["act"], db),
    )
    shards = lax.psum_scatter(grads, "dp", scatter_dimension=0, tiled=True)
    return (
        output.reshape(tokens.shape),
        input_grad.reshape(cotangent.shape),
        *(shard[None] for shard in shards),
    )


def solution(mesh):
    rows = P(("dp", "section"), None)
    layer = P("section", None)
    matrix = P("section", None, None)
    in_specs = (rows, rows, P("dp", None), layer, matrix, matrix, layer, matrix, matrix)
    split = P("section", "dp")
    split_matrix = P("section", "dp", None)
    out_specs = (rows, rows, split, split_matrix, split_matrix, split, split_matrix, split_matrix)
    return jax.shard_map(body, mesh=mesh, in_specs=in_specs, out_specs=out_specs, check_vma=False)
```

time: 3240 us -> 856 us (0.26)
  waiting for transfers between devices: 1520 us -> 463 us
  matrix products: 508 us -> 50.6 us
  other arithmetic: 411 us -> 0.8 us
  starting transfers between devices: 402 us -> 0.16 us
  local copies, waits for them, and re-layouts: 298 us -> 12.1 us
  Pallas kernels: 0 us -> 284 us
  loops' own time: 47.4 us -> 0 us
    ppermute x10 -> x0, waiting for transfers between devices: 912 us -> none  [passed_along(): return lax.ppermute(block, axis, route)]
    dot_general x52 -> x4, matrix products: 508 us -> 50.6 us  [matmul_lt(): lax.dot_general(left_side.reshape(rows, -1), right_side.reshape(rows, -1)...]
    ppermute x10 -> x0, starting transfers between devices: 402 us -> none  [passed_along(): return lax.ppermute(block, axis, route)]
    pallas_call x0 -> x2, Pallas kernels: none -> 284 us  [the longest x1 191 us: backward(): pl.pallas_call(functools.partial(backward_kernel, sections), out_shape=[s...]
    add x33 -> x1, other arithmetic: 167 us -> 0.77 us  [body(): docs = doc_ids + 1 + 16 * jnp.arange(rows, dtype=jnp.int32)[:, None]]
    reduce_scatter x6 -> x4, waiting for transfers between devices: 580 us -> 463 us  [body(): shards = lax.psum_scatter(grads, 'dp', scatter_dimension=0, tiled=True)]
    convert_element_type x12 -> x0, other arithmetic: 104 us -> none  [the longest x4 88.4 us: one_block(): grad_scores = (attn_probs * (grad_probs - inner_sum)).astype(jnp.bfloat16)]
    reduce_sum x17 -> x1, other arithmetic: 76 us -> 0.03 us  [body(): gains = jnp.sum(gains, axis=1)]
  transfers between devices with their start and end apart: 18 -> 4, of which waited for: 15 -> 3; matrix products, arithmetic and copies ran while one was open for 17% -> 5% of each run, Pallas kernels for 0% -> 0%
where the time goes in v1:
time: 856 us; the launch traced here: 848 us
  waiting for transfers between devices  463 us (54%)
  Pallas kernels  284 us (33%)
  matrix products  50.6 us (6%)
  blocking collectives  22.1 us (3%)
  between operations  14.9 us (2%)
  local copies, waits for them, and re-layouts  12.1 us (1%)
    reduce_scatter x4, waiting for transfers between devices, body(): shards = lax.psum_scatter(grads, 'dp', scatter_dimension=0, tiled=True)  463 us
    pallas_call x1, Pallas kernels, backward(): pl.pallas_call(functools.partial(backward_kernel, sections), out_shape=[s...  191 us
    pallas_call x1, Pallas kernels, forward(): pl.pallas_call(functools.partial(forward_kernel, sections), out_shape=[sd...  93.1 us
    dot_general x4, matrix products, matmul_lt(): lax.dot_general(left_side.reshape(rows, -1), right_side.reshape(rows, -1)...  50.6 us
    unnamed x1, blocking collectives  22.1 us
  transfers between devices with their start and end apart: 4, of which 3 were waited for; matrix products, arithmetic and copies ran while one was open for 5% of the time, Pallas kernels for 0%

profile of v1, /device:TPU:0, one launch (start us, length us, event | category | flops | bytes accessed | tf_op | source)
XLA Modules:
  0.0 847.7 jit_solution(15140497602225045250)
XLA Ops:
  7.2 0.0 reduce-scatter.7.cloned.1.call-start
  7.2 0.8 add_add_fusion
  8.0 1.9 broadcast_in_dim_reshape.8.doc_q
  9.9 0.6 broadcast_in_dim_reshape.7.doc_qr
  10.5 0.6 broadcast_in_dim.26.doc_k
  11.1 1.6 copy.29.doc_kc
  12.7 93.1 %layer_forward.1 = (bf16[2,256,768]{2,1,0:T(8,128)(2,1)}, bf16[8,256,768]{2,1,0:T(8,128)(2,1)}, bf16[8,256,768]{2,1,0:T(8,128)(2,1)}, bf16[8,256,768]{2,1,0:T(8,...) custom-call(bf16[2,256,768]{2,1,0:T(8,128)(2,1)} %bitcast.47, ...), custom_call_target="tpu_custom_call" | custom-call | tf_op jit(solution)/shard_map/layer_forward/pallas_call | solution.py:527
  105.8 0.0 copy-start
  105.8 191.0 %layer_backward.1 = (bf16[2,256,768]{2,1,0:T(8,128)(2,1)}, f32[2,8,768]{2,1,0:T(8,128)}, bf16[8,256,768]{2,1,0:T(8,128)(2,1)}, bf16[8,256,3072]{2,1,0:T(8,128)(2...) custom-call(bf16[2,256,768]{2,1,0:T(8,128)(2,1)} %bitcast.50, ...), custom_call_target="tpu_custom_call" | custom-call | tf_op jit(solution)/shard_map/layer_backward/pallas_call | solution.py:561
  296.8 5.9 convolution_bitcast_fusion.3
  302.8 0.0 reduce-scatter.7.cloned.1.call-update
  302.8 0.0 reduce-scatter.5.cloned.1.call-start
  302.9 13.9 %convolution_bitcast_fusion.1 = f32[768,2304]{1,0:T(8,128)} fusion(bf16[8,256,768]{2,1,0:T(8,128)(2,1)} %get-tuple-element.37, bf16[8,256,2304]{2,1,0:T(8,128)(2,1)} %get-tuple-element.38), kind=kOutput, calls=%fused_computation.1 | convolution fusion | flops 7247757312 | bytes 19660800 | tf_op jit(solution)/shard_map/dot_general | solution.py:604
  316.8 0.0 reduce-scatter.5.cloned.1.call-update
  316.8 0.0 reduce-scatter.11.cloned.1.call-start
  316.8 1.8 copy-done.5
  318.7 15.2 %convolution_bitcast_fusion = f32[3072,768]{1,0:T(8,128)} fusion(bf16[8,256,3072]{2,1,0:T(8,128)(2,1)} %get-tuple-element.42, bf16[8,256,768]{2,1,0:T(8,128)(2,1)S(1)} %copy-done.5), kind=kOutput, calls=%fused_computation | convolution fusion | flops 9663676416 | bytes 25165824 | tf_op jit(solution)/shard_map/dot_general | solution.py:604
  333.9 0.0 reduce-scatter.11.cloned.1.call-update
  333.9 0.0 reduce-scatter.9.cloned.1.call-start
  334.0 1.9 copy-done.4
  335.8 15.6 %convolution_bitcast_fusion.2 = f32[768,3072]{1,0:T(8,128)} fusion(bf16[8,256,768]{2,1,0:T(8,128)(2,1)S(1)} %copy-done.4, bf16[8,256,3072]{2,1,0:T(8,128)(2,1)} %get-tuple-element.41), kind=kOutput, calls=%fused_computation.2 | convolution fusion | flops 9663676416 | bytes 25165824 | tf_op jit(solution)/shard_map/dot_general | solution.py:604
  351.4 0.0 reduce-scatter.9.cloned.1.call-update
  351.4 0.8 copy-done.3
  352.2 0.0 copy-done.6
  352.2 0.6 dynamic-slice
  353.5 22.1 %all-reduce.3 = (f32[768]{0:T(1024)S(1)}, f32[768]{0:T(1024)S(1)}) all-reduce(f32[768]{0:T(1024)S(1)} %get-tuple-element.45, f32[768]{0:T(1024)S(1)} %get-tuple-element.44), channel_id=2, replica_groups=mesh['dp'=8,'section'=4] {'dp'}, use_global_device_ids=true, to_apply=%region_1.0.clone | all-reduce | flops 1536 | bytes 12288
  375.6 0.6 dynamic-slice_bitcast_fusion
  376.2 128.9 %reduce-scatter.5.cloned.1.call-done = f32[96,2304]{1,0:T(8,128)} async-done(((f32[768,2304]{1,0:T(8,128)}), f32[96,2304]{1,0:T(8,128)}) %reduce-scatter.5.cloned.1.call-update) | async-done | bytes 884752 | tf_op jit(solution)/shard_map/reduce_scatter | solution.py:633
  505.0 167.0 %reduce-scatter.11.cloned.1.call-done = f32[384,768]{1,0:T(8,128)} async-done(((f32[3072,768]{1,0:T(8,128)}), f32[384,768]{1,0:T(8,128)}) %reduce-scatter.11.cloned.1.call-update) | async-done | bytes 1179664 | tf_op jit(solution)/shard_map/reduce_scatter | solution.py:633
  672.0 166.9 %reduce-scatter.9.cloned.1.call-done = f32[96,3072]{1,0:T(8,128)} async-done(((f32[768,3072]{1,0:T(8,128)}), f32[96,3072]{1,0:T(8,128)}) %reduce-scatter.9.cloned.1.call-update) | async-done | bytes 1179664 | tf_op jit(solution)/shard_map/reduce_scatter | solution.py:633
  838.9 0.9 copy.40
  839.8 0.9 copy.41
  (15 shorter events, 0.1 us)
Async XLA Ops:
  7.2 369.0 %reduce-scatter.7.cloned.1.call-start = ((), (), s32[]{:S(2)}) async-start(), calls=%async_computation.5 | async-start | bytes 2654208 | tf_op jit(solution)/shard_map/reduce_scatter | solution.py:633
  105.8 191.0 %copy-start = (bf16[8,256,768]{2,1,0:T(8,128)(2,1)S(1)}, bf16[8,256,768]{2,1,0:T(8,128)(2,1)}, u32[]{:S(2)}) copy-start(bf16[8,256,768]{2,1,0:T(8,128)(2,1)} %get-tuple-element.31.s_mixed) | copy-start | bytes 9437188
  302.8 202.2 %reduce-scatter.5.cloned.1.call-start = ((), (), s32[]{:S(2)}) async-start(), calls=%async_computation.4 | async-start | bytes 7962624 | tf_op jit(solution)/shard_map/reduce_scatter | solution.py:633
  316.8 1.9 copy-start.5
  316.8 355.2 %reduce-scatter.11.cloned.1.call-start = ((), (), s32[]{:S(2)}) async-start(), calls=%async_computation.7 | async-start | bytes 10616832 | tf_op jit(solution)/shard_map/reduce_scatter | solution.py:633
  333.9 1.9 copy-start.4
  333.9 505.0 %reduce-scatter.9.cloned.1.call-start = ((), (), s32[]{:S(2)}) async-start(), calls=%async_computation.6 | async-start | bytes 10616832 | tf_op jit(solution)/shard_map/reduce_scatter | solution.py:633
  351.4 0.8 copy-start.3
  351.4 0.8 copy-start.6
  351.4 487.6 %copy-start.1 = (bf16[2,256,768]{2,1,0:T(8,128)(2,1)S(1)}, bf16[2,256,768]{2,1,0:T(8,128)(2,1)}, u32[]{:S(2)}) copy-start(bf16[2,256,768]{2,1,0:T(8,128)(2,1)} %get-tuple-element.26) | copy-start | bytes 2359300
  351.4 488.4 %copy-start.2 = (bf16[2,256,768]{2,1,0:T(8,128)(2,1)S(1)}, bf16[2,256,768]{2,1,0:T(8,128)(2,1)}, u32[]{:S(2)}) copy-start(bf16[2,256,768]{2,1,0:T(8,128)(2,1)} %get-tuple-element.35) | copy-start | bytes 2359300
Sparse Core Ops, SparseCore 0:
  302.9 69.7 reduce-scatter.6
  377.0 128.0 reduce-scatter.4
  509.6 162.3 reduce-scatter.10
  676.5 162.3 reduce-scatter.8

commit v2 on v1

--- a/solution.py
+++ b/solution.py
@@ -609,6 +609,278 @@
     )
 
 
+UNIT = 256
+UNITS = 9 + 3 + 12 + 12
+NARROW = 9 + 3 + 12
+X_LAG = 4
+Z_LAG = 6
+
+
+def dot_tn(a, b):
+    return lax.dot_general(a, b, (((0,), (0,)), ((), ())), preferred_element_type=F32)
+
+
+def weight_grad_kernel(
+    s_na,
+    s_dt,
+    s_mixed,
+    s_da,
+    s_nm,
+    s_dh,
+    s_act,
+    s_db,
+    gains,
+    o_qkv,
+    o_out,
+    o_up,
+    o_down,
+    o_gains,
+    left,
+    right,
+    act,
+    made,
+    from_x,
+    from_z,
+    total,
+    gain_own,
+    gain_in,
+    left_sems,
+    right_sems,
+    act_sem,
+    x_sends,
+    x_arrivals,
+    z_sends,
+    z_arrivals,
+    out_sem,
+    gain_sends,
+    gain_arrivals,
+):
+    section = lax.axis_index("section")
+    dp = lax.axis_index("dp")
+    x, z = lax.rem(dp, 2), dp // 2
+    partner = dp + 1 - 2 * x
+
+    def load_left(src, slot):
+        return pltpu.make_async_copy(src, left.at[slot], left_sems.at[slot])
+
+    def load_right(src, column, slot):
+        columns = pl.ds(pl.multiple_of(column * UNIT, UNIT), UNIT)
+        return pltpu.make_async_copy(src.at[:, columns], right.at[slot], right_sems.at[slot])
+
+    def start_right(unit):
+        slot = lax.rem(unit, 2)
+
+        @pl.when(unit < 9)
+        def _():
+            load_right(s_dt, unit, slot).start()
+
+        @pl.when((unit >= 9) & (unit < 12))
+        def _():
+            load_right(s_da, unit - 9, slot).start()
+
+        @pl.when((unit >= 12) & (unit < NARROW))
+        def _():
+            load_right(s_dh, unit - 12, slot).start()
+
+    load_left(s_na, 0).start()
+    start_right(0)
+    load_left(s_mixed, 1).start()
+    pltpu.make_async_copy(s_act, act, act_sem).start()
+    gain_own[...] = jnp.sum(gains[...], axis=1, keepdims=True) + jnp.zeros((2, 8, D), F32)
+
+    barrier = pltpu.get_barrier_semaphore()
+    for step in range(1, 8):
+        other = lax.rem(dp + step, 8)
+        pl.semaphore_signal(barrier, inc=1, device_id=(other, section), device_id_type=MESH)
+    pl.semaphore_wait(barrier, 7)
+
+    def gain_copy(step):
+        other = lax.rem(dp + step, 8)
+        return pltpu.make_async_remote_copy(
+            gain_own,
+            gain_in.at[step - 1],
+            gain_sends.at[step - 1],
+            gain_arrivals.at[step - 1],
+            device_id=(other, section),
+            device_id_type=MESH,
+        )
+
+    for step in range(1, 8):
+        gain_copy(step).start()
+
+    def send_x(unit):
+        pltpu.make_async_remote_copy(
+            made.at[unit, 1 - x],
+            from_x.at[unit],
+            x_sends.at[unit],
+            x_arrivals.at[unit],
+            device_id=(partner, section),
+            device_id_type=MESH,
+        ).start()
+
+    def send_z(unit, step):
+        target = lax.rem(z + step, 4)
+        pltpu.make_async_remote_copy(
+            made.at[unit, x, target],
+            from_z.at[unit, 3 - step],
+            z_sends.at[unit],
+            z_arrivals.at[unit],
+            device_id=(target * 2 + x, section),
+            device_id_type=MESH,
+        ).start()
+
+    def deliver(unit):
+        for first, end, ref in ((0, 9, o_qkv), (9, 12, o_out), (12, NARROW, o_up)):
+
+            @pl.when((unit >= first) & (unit < end))
+            def _():
+                columns = pl.ds(pl.multiple_of((unit - first) * UNIT, UNIT), UNIT)
+                pltpu.make_async_copy(total.at[unit], ref.at[:, columns], out_sem).start()
+
+        @pl.when(unit >= NARROW)
+        def _():
+            column, row = (unit - NARROW) // 4, lax.rem(unit - NARROW, 4)
+            columns = pl.ds(pl.multiple_of(column * UNIT, UNIT), UNIT)
+            rows = pl.ds(pl.multiple_of(row * 96, 96), 96)
+            pltpu.make_async_copy(total.at[unit], o_down.at[rows, columns], out_sem).start()
+
+    def advance(now):
+        @pl.when((now >= X_LAG) & (now - X_LAG < UNITS))
+        def _():
+            unit = now - X_LAG
+            await_arrival(from_x.at[unit], x_arrivals.at[unit])
+            made[unit, x] = (made[unit, x].astype(F32) + from_x[unit].astype(F32)).astype(BF16)
+            for step in range(1, 4):
+                send_z(unit, step)
+
+        @pl.when((now >= Z_LAG) & (now - Z_LAG < UNITS))
+        def _():
+            unit = now - Z_LAG
+            await_arrival(from_z.at[unit], z_arrivals.at[unit])
+            got = from_z[unit].astype(F32)
+            total[unit] = made[unit, x, z].astype(F32) + got[0] + got[1] + got[2]
+            deliver(unit)
+
+    def narrow(unit, carry):
+        slot = lax.rem(unit, 2)
+        side = jnp.where((unit >= 9) & (unit < 12), 1, 0)
+
+        @pl.when(unit == 9)
+        def _():
+            load_left(s_nm, 0).start()
+
+        @pl.when(unit == 12)
+        def _():
+            load_left(s_db, 1).start()
+
+        start_right(unit + 1)
+
+        @pl.when((unit == 0) | (unit == 12))
+        def _():
+            load_left(s_na, 0).wait()
+
+        @pl.when(unit == 9)
+        def _():
+            load_left(s_mixed, 1).wait()
+
+        load_right(s_dt, 0, slot).wait()
+        grad = dot_tn(left[side], right[slot]).astype(BF16)
+        for shard in range(8):
+            made[unit, shard % 2, shard // 2] = grad[shard * 96 : (shard + 1) * 96]
+        send_x(unit)
+        advance(unit)
+        return carry
+
+    lax.fori_loop(0, NARROW, narrow, 0)
+    load_left(s_db, 1).wait()
+    pltpu.make_async_copy(s_act, act, act_sem).wait()
+
+    def wide(step, carry):
+        column, shard = step // 8, lax.rem(step, 8)
+        columns = pl.ds(pl.multiple_of(column * UNIT, UNIT), UNIT)
+        rows = pl.ds(pl.multiple_of(shard * 384, 384), 384)
+        grad = dot_tn(act[:, rows], left[1, :, columns]).astype(BF16)
+        first = NARROW + 4 * column
+        for part in range(4):
+            made[first + part, lax.rem(shard, 2), shard // 2] = grad[part * 96 : (part + 1) * 96]
+
+        @pl.when(shard == 7)
+        def _():
+            for part in range(4):
+                send_x(first + part)
+
+        @pl.when(lax.rem(step, 2) == 1)
+        def _():
+            advance(NARROW + step // 2)
+
+        return carry
+
+    lax.fori_loop(0, 24, wide, 0)
+
+    def drain(now, carry):
+        advance(now)
+        return carry
+
+    lax.fori_loop(UNITS, UNITS + Z_LAG, drain, 0)
+    for step in range(1, 8):
+        gain_copy(step).wait()
+    sums = gain_own[:, 0:1]
+    for step in range(7):
+        sums = sums + gain_in[step, :, 0:1]
+    o_gains[...] = sums
+
+    def sent(unit, carry):
+        await_arrival(from_x.at[unit], x_sends.at[unit])
+        await_arrival(from_z.at[unit], z_sends.at[unit])
+        return carry
+
+    lax.fori_loop(0, UNITS, sent, 0)
+    await_arrival(total, out_sem)
+
+
+def weight_grads(na, dt, mixed, da, nm, dh, act, db, gains):
+    tokens = na.shape[0] * na.shape[1]
+    sds = jax.ShapeDtypeStruct
+    operands = [v.reshape(tokens, -1) for v in (na, dt, mixed, da, nm, dh, act, db)]
+    return pl.pallas_call(
+        weight_grad_kernel,
+        out_shape=[
+            sds((96, 3 * D), F32),
+            sds((96, D), F32),
+            sds((96, FF), F32),
+            sds((384, D), F32),
+            sds((2, 1, D), F32),
+        ],
+        in_specs=[ANY] * 8 + [IN_VMEM],
+        out_specs=[ANY] * 4 + [IN_VMEM],
+        scratch_shapes=[
+            pltpu.VMEM((2, tokens, D), BF16),
+            pltpu.VMEM((2, tokens, UNIT), BF16),
+            pltpu.VMEM((tokens, FF), BF16),
+            pltpu.VMEM((UNITS, 2, 4, 96, UNIT), BF16),
+            pltpu.VMEM((UNITS, 4, 96, UNIT), BF16),
+            pltpu.VMEM((UNITS, 3, 96, UNIT), BF16),
+            pltpu.VMEM((UNITS, 96, UNIT), F32),
+            pltpu.VMEM((2, 8, D), F32),
+            pltpu.VMEM((7, 2, 8, D), F32),
+            DMA((2,)),
+            DMA((2,)),
+            DMA,
+            DMA((UNITS,)),
+            DMA((UNITS,)),
+            DMA((UNITS,)),
+            DMA((UNITS,)),
+            DMA,
+            DMA((7,)),
+            DMA((7,)),
+        ],
+        compiler_params=pltpu.CompilerParams(
+            collective_id=2, has_side_effects=True, vmem_limit_bytes=VMEM_LIMIT
+        ),
+        name="weight_grads",
+    )(*operands, gains)
+
+
 def body(tokens, cotangent, doc_ids, gain_attn, w_qkv, w_out, gain_mlp, w_up, w_down):
     sections = lax.axis_size("section")
     rows, seq = doc_ids.shape
@@ -621,16 +893,23 @@
     input_grad, gains, db, dh, da, dt = backward(
         sections, chunks, cotangent, docs_q[:, None, :], docs_k[:, :, None], weights, kept
     )
-    gains = jnp.sum(gains, axis=1)
-    grads = (
-        gains[0],
-        matmul_lt(kept["na"], dt),
-        matmul_lt(kept["mixed"], da),
-        gains[1],
-        matmul_lt(kept["nm"], dh),
-        matmul_lt(kept["act"], db),
-    )
-    shards = lax.psum_scatter(grads, "dp", scatter_dimension=0, tiled=True)
+    if lax.axis_size("dp") == 8 and chunks == 8:
+        qkv, out, up, down, gains = weight_grads(
+            kept["na"], dt, kept["mixed"], da, kept["nm"], dh, kept["act"], db, gains
+        )
+        gains = lax.dynamic_slice(gains, (0, 0, lax.axis_index("dp") * 96), (2, 1, 96))
+        shards = (gains[0, 0], qkv, out, gains[1, 0], up, down)
+    else:
+        gains = jnp.sum(gains, axis=1)
+        grads = (
+            gains[0],
+            matmul_lt(kept["na"], dt),
+            matmul_lt(kept["mixed"], da),
+            gains[1],
+            matmul_lt(kept["nm"], dh),
+            matmul_lt(kept["act"], db),
+        )
+        shards = lax.psum_scatter(grads, "dp", scatter_dimension=0, tiled=True)
     return (
         output.reshape(tokens.shape),
         input_grad.reshape(cotangent.shape),

time: 856 us -> 459 us (0.54)
  waiting for transfers between devices: 463 us -> 0 us
  Pallas kernels: 284 us -> 445 us
  matrix products: 50.6 us -> 0 us
  blocking collectives: 22.1 us -> 0 us
  between operations: 14.9 us -> 0.71 us
    reduce_scatter x4 -> x0, waiting for transfers between devices: 463 us -> none  [body(): shards = lax.psum_scatter(grads, 'dp', scatter_dimension=0, tiled=True)]
    pallas_call x0 -> x1, Pallas kernels: none -> 161 us  [weight_grads(): pl.pallas_call(weight_grad_kernel, out_shape=[sds((96, 3 * D), F32), sds(...]
    dot_general x4 -> x0, matrix products: 50.6 us -> none  [matmul_lt(): lax.dot_general(left_side.reshape(rows, -1), right_side.reshape(rows, -1)...]
    unnamed x1 -> x0, blocking collectives: 22.1 us -> none
  transfers between devices with their start and end apart: 4 -> 0, of which waited for: 3 -> 0; matrix products, arithmetic and copies ran while one was open for 5% -> 0% of each run, Pallas kernels for 0% -> 0%
where the time goes in v2:
time: 459 us
  Pallas kernels  445 us (97%)
  local copies, waits for them, and re-layouts  12.8 us (3%)
    pallas_call x1, Pallas kernels, backward(): pl.pallas_call(functools.partial(backward_kernel, sections), out_shape=[s...  191 us
    pallas_call x1, Pallas kernels, weight_grads(): pl.pallas_call(weight_grad_kernel, out_shape=[sds((96, 3 * D), F32), sds(...  161 us
    pallas_call x1, Pallas kernels, forward(): pl.pallas_call(functools.partial(forward_kernel, sections), out_shape=[sd...  93.1 us

profile of v2, /device:TPU:0, one launch (start us, length us, event | category | flops | bytes accessed | tf_op | source)
XLA Modules:
  0.0 459.0 jit_solution(15786710838005682702)
XLA Ops:
  0.6 0.8 add_add_fusion
  1.4 0.6 broadcast_in_dim.20.doc_k
  2.0 1.9 broadcast_in_dim_reshape.8.doc_q
  4.0 93.1 %layer_forward.1 = (bf16[2,256,768]{2,1,0:T(8,128)(2,1)}, bf16[8,256,768]{2,1,0:T(8,128)(2,1)}, bf16[8,256,768]{2,1,0:T(8,128)(2,1)}, bf16[8,256,768]{2,1,0:T(8,...) custom-call(bf16[2,256,768]{2,1,0:T(8,128)(2,1)} %bitcast.49, ...), custom_call_target="tpu_custom_call" | custom-call | tf_op jit(solution)/shard_map/layer_forward/pallas_call | solution.py:527
  97.0 1.5 copy.19.doc_kc
  98.6 0.6 broadcast_in_dim_reshape.7.doc_qr
  99.2 190.7 %layer_backward.1 = (bf16[2,256,768]{2,1,0:T(8,128)(2,1)}, f32[2,8,768]{2,1,0:T(8,128)}, bf16[8,256,768]{2,1,0:T(8,128)(2,1)}, bf16[8,256,3072]{2,1,0:T(8,128)(2...) custom-call(bf16[2,256,768]{2,1,0:T(8,128)(2,1)} %bitcast.52, ...), custom_call_target="tpu_custom_call" | custom-call | tf_op jit(solution)/shard_map/layer_backward/pallas_call | solution.py:561
  289.9 0.0 copy-start.3
  289.9 161.0 %weight_grads.1 = (f32[96,2304]{1,0:T(8,128)}, f32[96,768]{1,0:T(8,128)}, f32[96,3072]{1,0:T(8,128)}, f32[384,768]{1,0:T(8,128)}, f32[2,1,768]{2,1,0:T(1,128)}) custom-call(bf16[2048,768]{1,0:T(8,128)(2,1)} %bitcast.40, bf16[2048,2304]{1,0:T(8,128)(2,1)} %bitcast.37, bf16[2048,768]{1,0:T(8,128)(2,1)} %bitcast.34, bf16[2048,768]{1,0:T(8,128)(2,1)} %bitcast.45, ...), custom_call_target="tpu_custom_call" | custom-call | tf_op jit(solution)/shard_map/weight_grads/pallas_call | solution.py:845
  450.9 0.0 copy-start.2
  450.9 0.0 copy-start.4
  450.9 0.0 copy-start.1
  450.9 1.4 dynamic-slice_bitcast_fusion
  452.3 0.0 copy-done.3
  452.3 0.9 copy.26
  453.2 0.0 copy-start
  453.2 2.2 copy.27
  455.4 0.0 copy-done.2
  455.4 0.9 copy.28
  456.3 0.0 copy-done.4
  456.3 0.7 copy.29
  457.0 0.0 copy-done.1
  457.0 1.0 copy.30
  458.0 0.0 copy-done
  458.0 1.0 copy.31
  (3 shorter events, 0.0 us)
Async XLA Ops:
  289.9 162.5 %copy-start.3 = (bf16[2,256,768]{2,1,0:T(8,128)(2,1)S(1)}, bf16[2,256,768]{2,1,0:T(8,128)(2,1)}, u32[]{:S(2)}) copy-start(bf16[2,256,768]{2,1,0:T(8,128)(2,1)} %get-tuple-element.31) | copy-start | bytes 2359300
  450.9 4.5 copy-start.2
  450.9 5.4 %copy-start.4 = (f32[96,768]{1,0:T(8,128)S(1)}, f32[96,768]{1,0:T(8,128)}, u32[]{:S(2)}) copy-start(f32[96,768]{1,0:T(8,128)} %get-tuple-element.51) | copy-start | bytes 884740
  450.9 6.1 %copy-start.1 = (f32[96,3072]{1,0:T(8,128)S(1)}, f32[96,3072]{1,0:T(8,128)}, u32[]{:S(2)}) copy-start(f32[96,3072]{1,0:T(8,128)} %get-tuple-element.52) | copy-start | bytes 3538948
  453.2 4.8 %copy-start = (f32[384,768]{1,0:T(8,128)S(1)}, f32[384,768]{1,0:T(8,128)}, u32[]{:S(2)}) copy-start(f32[384,768]{1,0:T(8,128)} %get-tuple-element.53) | copy-start | bytes 3538948

commit v3 on v2

--- a/solution.py
+++ b/solution.py
@@ -139,17 +139,57 @@
             await_arrival(result.at[piece], kept.at[piece])
 
 
+def fill_bias(docs, chunk, bias, keys_down):
+    per_row = docs.shape[1] // C
+    row, place = chunk // per_row, lax.rem(chunk, per_row)
+
+    def numbers(block):
+        start = pl.multiple_of(jnp.maximum(block, 0) * C, C)
+        return docs[pl.ds(row, 1), pl.ds(start, C)].astype(F32)
+
+    def upright(line):
+        return jnp.transpose(jnp.broadcast_to(line, (128, C)))
+
+    queries = numbers(place)
+    if not keys_down:
+        queries = upright(queries)
+    for part in range(WIN):
+        keys = numbers(place - (WIN - 1) + part)
+        if keys_down:
+            keys = upright(keys)
+        for half in range(C // 128):
+            lanes = slice(half * 128, (half + 1) * 128)
+            allowed = keys == queries[:, lanes] if keys_down else queries == keys[:, lanes]
+            if part == WIN - 1:
+                down = lax.broadcasted_iota(jnp.int32, (C, 128), 0)
+                across = lax.broadcasted_iota(jnp.int32, (C, 128), 1) + half * 128
+                allowed = allowed & ((down <= across) if keys_down else (across <= down))
+            term = jnp.where(allowed, 0.0, NEG)
+            if keys_down:
+                bias[part * C : (part + 1) * C, lanes] = term
+            else:
+                bias[:, part * C + half * 128 : part * C + (half + 1) * 128] = term
+
+
+def by_blocks(docs, chunk, attend):
+    place = lax.rem(chunk, docs.shape[1] // C)
+    for blocks in range(1, WIN + 1):
+
+        @pl.when((place == blocks - 1) if blocks < WIN else (place >= WIN - 1))
+        def _():
+            attend(blocks)
+
+
 def forward_kernel(
     sections,
     tokens,
-    doc_q,
-    doc_k,
+    docs,
     gain_a,
     gain_m,
-    w_qkv,
-    w_out,
-    w_up,
-    w_down,
+    h_qkv,
+    h_out,
+    h_up,
+    h_down,
     result,
     s_x,
     s_q,
@@ -162,6 +202,10 @@
     s_nm,
     s_act,
     s_dg,
+    w_qkv,
+    w_out,
+    w_up,
+    w_down,
     inbox,
     outbox,
     kbuf,
@@ -181,19 +225,32 @@
     landed,
     kept,
     saves,
+    weight_sems,
 ):
     section = lax.axis_index("section")
     chunks = inbox.shape[0]
     per = tokens.shape[0]
+    weights = [
+        pltpu.make_async_copy(src, dst, weight_sems.at[kind])
+        for kind, (src, dst) in enumerate(
+            ((h_qkv, w_qkv), (h_out, w_out), (h_up, w_up), (h_down, w_down))
+        )
+    ]
+    for copy in weights:
+        copy.start()
+
+    def at_first(chunk, copy):
+        @pl.when(chunk == 0)
+        def _():
+            copy.wait()
+
     greet(section, sections)
     scatter_rows(section, sections, per, tokens, inbox, arrivals, first_sends, 0)
     low, high, is_low = lane_masks()
-    kbuf[pl.ds(0, 2 * C), :] = jnp.zeros((2 * C, D), BF16)
-    vbuf[pl.ds(0, 2 * C), :] = jnp.zeros((2 * C, D), BF16)
     centered = jnp.where(section == 0, 1.0, 0.0).astype(F32)
 
     def stores(chunk, slot):
-        here = pl.ds(pl.multiple_of((chunk + 2) * C, C), C)
+        here = pl.ds(pl.multiple_of(chunk * C, C), C)
         pairs = (
             (inbox.at[chunk], s_x),
             (kbuf.at[here], s_k),
@@ -221,6 +278,8 @@
                 copy.wait()
 
         todo = stores(chunk, slot)
+        at_first(chunk, weights[0])
+        fill_bias(docs, chunk, bias, False)
         await_arrival(inbox.at[chunk], arrivals.at[chunk])
         todo[0].start()
         x = inbox[chunk].astype(F32)
@@ -229,38 +288,37 @@
         b_na[slot] = na
         todo[4].start()
         b_q[slot] = (dot(na, w_qkv[:, :D]).astype(BF16) * (HD**-0.5)).astype(BF16)
-        here = pl.ds(pl.multiple_of((chunk + 2) * C, C), C)
+        here = pl.ds(pl.multiple_of(chunk * C, C), C)
         kbuf[here, :] = dot(na, w_qkv[:, D : 2 * D]).astype(BF16)
         vbuf[here, :] = dot(na, w_qkv[:, 2 * D :]).astype(BF16)
         todo[1].start()
         todo[2].start()
         todo[3].start()
-        for part in range(WIN):
-            allowed = doc_q[chunk] == doc_k[chunk + part]
-            if part == WIN - 1:
-                row = lax.broadcasted_iota(jnp.int32, (C, C), 0)
-                col = lax.broadcasted_iota(jnp.int32, (C, C), 1)
-                allowed = allowed & (col <= row)
-            bias[:, part * C : (part + 1) * C] = jnp.where(allowed, 0.0, NEG)
-        window = pl.ds(pl.multiple_of(chunk * C, C), WIN * C)
         lane = lax.broadcasted_iota(jnp.int32, (1, 128), 1)
-        lse_all = jnp.zeros((C, 128), F32)
-        for pair in range(PAIRS):
-            lanes = slice(pair * 2 * HD, (pair + 1) * 2 * HD)
-            q2 = two_heads(b_q[slot, :, lanes], low, high)
-            s = dot_nt(q2, kbuf[window, lanes]).reshape(2, C, WIN * C) + bias[...][None]
-            top = jnp.max(s, axis=-1, keepdims=True)
-            e = jnp.exp(s - top)
-            total = jnp.sum(e, axis=-1, keepdims=True)
-            o = dot(e.astype(BF16).reshape(2 * C, WIN * C), vbuf[window, lanes])
-            o = o.reshape(2, C, 2 * HD) * (1.0 / total)
-            b_mixed[slot, :, lanes] = jnp.where(is_low, o[0], o[1]).astype(BF16)
-            lse = top + jnp.log(total)
-            lse_all = jnp.where(lane == 2 * pair, lse[0], lse_all)
-            lse_all = jnp.where(lane == 2 * pair + 1, lse[1], lse_all)
-        b_lse[slot] = jnp.transpose(lse_all)[:16]
+
+        def attend(blocks):
+            window = pl.ds(pl.multiple_of((chunk - blocks + 1) * C, C), blocks * C)
+            masked = slice((WIN - blocks) * C, WIN * C)
+            lse_all = jnp.zeros((C, 128), F32)
+            for pair in range(PAIRS):
+                lanes = slice(pair * 2 * HD, (pair + 1) * 2 * HD)
+                q2 = two_heads(b_q[slot, :, lanes], low, high)
+                s = dot_nt(q2, kbuf[window, lanes]).reshape(2, C, blocks * C) + bias[:, masked][None]
+                top = jnp.max(s, axis=-1, keepdims=True)
+                e = jnp.exp(s - top)
+                total = jnp.sum(e, axis=-1, keepdims=True)
+                o = dot(e.astype(BF16).reshape(2 * C, blocks * C), vbuf[window, lanes])
+                o = o.reshape(2, C, 2 * HD) * (1.0 / total)
+                b_mixed[slot, :, lanes] = jnp.where(is_low, o[0], o[1]).astype(BF16)
+                lse = top + jnp.log(total)
+                lse_all = jnp.where(lane == 2 * pair, lse[0], lse_all)
+                lse_all = jnp.where(lane == 2 * pair + 1, lse[1], lse_all)
+            b_lse[slot] = jnp.transpose(lse_all)[:16]
+
+        by_blocks(docs, chunk, attend)
         todo[5].start()
         todo[6].start()
+        at_first(chunk, weights[1])
         branch = dot(b_mixed[slot], w_out[...])
         mid = x + branch - row_mean(branch)
         b_mid[slot] = mid
@@ -268,6 +326,7 @@
         nm = (mid * lax.rsqrt(row_mean(mid * mid) + EPS) * gain_m[...]).astype(BF16)
         b_nm[slot] = nm
         todo[8].start()
+        at_first(chunk, weights[2])
         k0 = 0.7978845608028654
         k1 = 0.044715
         for part in range(FF // D):
@@ -281,6 +340,7 @@
             b_dg[slot, :, cols] = slope.astype(BF16)
         todo[9].start()
         todo[10].start()
+        at_first(chunk, weights[3])
         branch = dot(b_act[slot], w_down[...])
         outbox[chunk] = (b_mid[slot] + branch - row_mean(branch)).astype(BF16)
         pass_on(section, chunk, per, sections - 1, 1, outbox, inbox, result, sends, arrivals, landed, kept)
@@ -297,14 +357,13 @@
 def backward_kernel(
     sections,
     cotangent,
-    doc_qr,
-    doc_kc,
+    docs,
     gain_a,
     gain_m,
-    w_qkv,
-    w_out,
-    w_up,
-    w_down,
+    h_qkv,
+    h_out,
+    h_up,
+    h_down,
     s_x,
     s_q,
     s_k,
@@ -319,6 +378,10 @@
     s_dh,
     s_da,
     s_dt,
+    w_qkv,
+    w_out,
+    w_up,
+    w_down,
     inbox,
     outbox,
     kbuf,
@@ -327,6 +390,7 @@
     dk_acc,
     dv_acc,
     lse_d,
+    b_dmix,
     marks,
     b_x,
     b_q,
@@ -346,6 +410,7 @@
     loads,
     saves,
     kv_sems,
+    weight_sems,
 ):
     section = lax.axis_index("section")
     chunks = inbox.shape[0]
@@ -374,26 +439,38 @@
         ]
 
     kv_copies = [
-        pltpu.make_async_copy(s_k, kbuf.at[pl.ds(2 * C, chunks * C)], kv_sems.at[0]),
-        pltpu.make_async_copy(s_v, vbuf.at[pl.ds(2 * C, chunks * C)], kv_sems.at[1]),
+        pltpu.make_async_copy(s_k, kbuf, kv_sems.at[0]),
+        pltpu.make_async_copy(s_v, vbuf, kv_sems.at[1]),
     ]
+    weights = [
+        pltpu.make_async_copy(src, dst, weight_sems.at[kind])
+        for kind, (src, dst) in enumerate(
+            ((h_down, w_down), (h_up, w_up), (h_out, w_out), (h_qkv, w_qkv))
+        )
+    ]
+    weights[0].start()
     for copy in fetches(chunks - 1, 0):
         copy.start()
+    weights[1].start()
+    weights[2].start()
     for copy in kv_copies:
         copy.start()
+    weights[3].start()
+
+    def at_first(step, copy):
+        @pl.when(step == 0)
+        def _():
+            copy.wait()
+
     greet(section, sections)
     scatter_rows(section, sections, per, cotangent, inbox, arrivals, first_sends, last)
     low, high, _ = lane_masks()
-    kbuf[pl.ds(0, 2 * C), :] = jnp.zeros((2 * C, D), BF16)
-    vbuf[pl.ds(0, 2 * C), :] = jnp.zeros((2 * C, D), BF16)
     dk_acc[...] = jnp.zeros_like(dk_acc)
     dv_acc[...] = jnp.zeros_like(dv_acc)
     gains[...] = jnp.zeros_like(gains)
     owner_of = lax.broadcasted_iota(jnp.int32, (D, 128), 0) // HD
     marks[...] = (owner_of == lax.broadcasted_iota(jnp.int32, (D, 128), 1)).astype(F32).astype(BF16)
     centered = jnp.where(section == 0, 1.0, 0.0).astype(F32)
-    for copy in kv_copies:
-        copy.wait()
 
     def folded(v):
         return jnp.sum(v.reshape(C // 8, 8, D), axis=0)
@@ -415,6 +492,8 @@
         for copy in fetches(chunk, slot):
             copy.wait()
         todo = stores(chunk, slot)
+        at_first(step, weights[0])
+        fill_bias(docs, chunk, bias, True)
         await_arrival(inbox.at[chunk], arrivals.at[chunk])
         g = inbox[chunk].astype(F32)
         db = (g - row_mean(g)).astype(BF16)
@@ -425,6 +504,7 @@
             d_active = dot_nt(db, w_down[cols, :])
             b_dh[slot, :, cols] = (d_active * b_dg[slot, :, cols].astype(F32)).astype(BF16)
         todo[1].start()
+        at_first(step, weights[1])
         dn = dot_nt(b_dh[slot], w_up[...])
         mid = b_mid[slot]
         factor = lax.rsqrt(row_mean(mid * mid) + EPS)
@@ -436,51 +516,51 @@
         b_da[slot] = da
         todo[2].start()
         b_mid[slot] = d_mid
+        at_first(step, weights[2])
         dmix = dot_nt(da, w_out[...]).astype(BF16)
+        b_dmix[...] = dmix
         prod = dmix.astype(F32) * b_mixed[slot].astype(F32)
         top = prod.astype(BF16)
         rest = (prod - top.astype(F32)).astype(BF16)
         inner = dot(top, marks[...]) + dot(rest, marks[...])
         lse_d[...] = jnp.transpose(inner)[:16]
-        for part in range(WIN):
-            allowed = doc_kc[chunk + part] == doc_qr[chunk]
-            if part == WIN - 1:
-                key = lax.broadcasted_iota(jnp.int32, (C, C), 0)
-                query = lax.broadcasted_iota(jnp.int32, (C, C), 1)
-                allowed = allowed & (key <= query)
-            bias[part * C : (part + 1) * C, :] = jnp.where(allowed, 0.0, NEG)
-        window = pl.ds(pl.multiple_of(chunk * C, C), WIN * C)
-        for pair in range(PAIRS):
-            lanes = slice(pair * 2 * HD, (pair + 1) * 2 * HD)
-            q2 = two_heads(b_q[slot, :, lanes], low, high)
-            do2 = two_heads(dmix[:, lanes], low, high)
-            keys = kbuf[window, lanes]
-            values = vbuf[window, lanes]
-            both = jnp.concatenate([bias[...], bias[...]], axis=1)
-            lse = jnp.concatenate(
-                [b_lse[slot, 2 * pair : 2 * pair + 1, :], b_lse[slot, 2 * pair + 1 : 2 * pair + 2, :]], axis=1
-            )
-            inner = jnp.concatenate(
-                [lse_d[2 * pair : 2 * pair + 1, :], lse_d[2 * pair + 1 : 2 * pair + 2, :]], axis=1
-            )
-            probs = jnp.exp(dot_nt(keys, q2) + both - lse)
-            ds = (probs * (dot_nt(values, do2) - inner)).astype(BF16)
-            dv = dot(probs.astype(BF16), do2)
-            dk = dot(ds, q2)
-            for part in range(WIN):
-                place = lax.rem(chunk + part, WIN)
-                rows = slice(part * C, (part + 1) * C)
-                dv_acc[place, :, lanes] += dv[rows]
-                dk_acc[place, :, lanes] += dk[rows]
-            dq = dot(jnp.transpose(keys), ds)
-            dq = jnp.concatenate([dq[:HD, :C], dq[HD:, C:]], axis=0)
-            b_dt[slot, :, lanes] = (jnp.transpose(dq) * (HD**-0.5)).astype(BF16)
-        done = lax.rem(chunk + WIN - 1, WIN)
+        for copy in kv_copies:
+            at_first(step, copy)
+
+        def attend(blocks):
+            window = pl.ds(pl.multiple_of((chunk - blocks + 1) * C, C), blocks * C)
+            masked = slice((WIN - blocks) * C, WIN * C)
+            for pair in range(PAIRS):
+                lanes = slice(pair * 2 * HD, (pair + 1) * 2 * HD)
+                q2 = two_heads(b_q[slot, :, lanes], low, high)
+                do2 = two_heads(b_dmix[:, lanes], low, high)
+                keys = kbuf[window, lanes]
+                values = vbuf[window, lanes]
+                both = jnp.concatenate([bias[masked, :], bias[masked, :]], axis=1)
+                even, odd = slice(2 * pair, 2 * pair + 1), slice(2 * pair + 1, 2 * pair + 2)
+                lse = jnp.concatenate([b_lse[slot, even, :], b_lse[slot, odd, :]], axis=1)
+                inner = jnp.concatenate([lse_d[even, :], lse_d[odd, :]], axis=1)
+                probs = jnp.exp(dot_nt(keys, q2) + both - lse)
+                ds = (probs * (dot_nt(values, do2) - inner)).astype(BF16)
+                dv = dot(probs.astype(BF16), do2)
+                dk = dot(ds, q2)
+                for part in range(blocks):
+                    place = lax.rem(chunk - blocks + 1 + part, WIN)
+                    rows = slice(part * C, (part + 1) * C)
+                    dv_acc[place, :, lanes] += dv[rows]
+                    dk_acc[place, :, lanes] += dk[rows]
+                dq = dot(jnp.transpose(keys), ds)
+                dq = jnp.concatenate([dq[:HD, :C], dq[HD:, C:]], axis=0)
+                b_dt[slot, :, lanes] = (jnp.transpose(dq) * (HD**-0.5)).astype(BF16)
+
+        by_blocks(docs, chunk, attend)
+        done = lax.rem(chunk, WIN)
         b_dt[slot, :, D : 2 * D] = dk_acc[done].astype(BF16)
         b_dt[slot, :, 2 * D :] = dv_acc[done].astype(BF16)
         dk_acc[done] = jnp.zeros((C, D), F32)
         dv_acc[done] = jnp.zeros((C, D), F32)
         todo[3].start()
+        at_first(step, weights[3])
         dn = dot_nt(b_dt[slot], w_qkv[...])
         x = b_x[slot].astype(F32)
         x = x - centered * row_mean(x)
@@ -507,7 +587,10 @@
 DMA = pltpu.SemaphoreType.DMA
 
 
-def forward(sections, chunks, tokens, doc_q, doc_k, weights):
+WEIGHTS = [pltpu.VMEM(shape, BF16) for shape in ((D, 3 * D), (D, D), (D, FF), (FF, D))]
+
+
+def forward(sections, chunks, tokens, docs, weights):
     per = chunks // sections
     sds = jax.ShapeDtypeStruct
     saved = (
@@ -527,26 +610,27 @@
     outs = pl.pallas_call(
         functools.partial(forward_kernel, sections),
         out_shape=[sds((per, C, D), BF16)] + [sds((chunks,) + s, t) for _, s, t in saved],
-        in_specs=[ANY] + [IN_VMEM] * 8,
+        in_specs=[ANY] + [IN_VMEM] * 3 + [ANY] * 4,
         out_specs=[ANY] * (1 + len(saved)),
-        scratch_shapes=[
+        scratch_shapes=WEIGHTS
+        + [
             pltpu.VMEM((chunks, C, D), BF16),
             pltpu.VMEM((chunks, C, D), BF16),
-            pltpu.VMEM(((chunks + 2) * C, D), BF16),
-            pltpu.VMEM(((chunks + 2) * C, D), BF16),
+            pltpu.VMEM((chunks * C, D), BF16),
+            pltpu.VMEM((chunks * C, D), BF16),
             pltpu.VMEM((C, WIN * C), F32),
         ]
         + [pltpu.VMEM((2,) + s, t) for _, s, t in staged]
-        + [DMA((chunks,)), DMA((chunks,)), DMA((per,)), DMA((per,)), DMA((per,)), DMA((11, 2))],
+        + [DMA((chunks,)), DMA((chunks,)), DMA((per,)), DMA((per,)), DMA((per,)), DMA((11, 2)), DMA((4,))],
         compiler_params=pltpu.CompilerParams(
             collective_id=0, has_side_effects=True, vmem_limit_bytes=VMEM_LIMIT
         ),
         name="layer_forward",
-    )(tokens.reshape(per, C, D), doc_q, doc_k, *weights)
+    )(tokens.reshape(per, C, D), docs, *weights)
     return outs[0], {name: out for (name, _, _), out in zip(saved, outs[1:])}
 
 
-def backward(sections, chunks, cotangent, doc_qr, doc_kc, weights, kept):
+def backward(sections, chunks, cotangent, docs, weights, kept):
     per = chunks // sections
     sds = jax.ShapeDtypeStruct
     fetched = (
@@ -561,31 +645,32 @@
     outs = pl.pallas_call(
         functools.partial(backward_kernel, sections),
         out_shape=[sds((per, C, D), BF16), sds((2, 8, D), F32)] + [sds((chunks,) + s, BF16) for s in saved],
-        in_specs=[ANY] + [IN_VMEM] * 8 + [ANY] * 8,
+        in_specs=[ANY] + [IN_VMEM] * 3 + [ANY] * 12,
         out_specs=[ANY, IN_VMEM] + [ANY] * len(saved),
-        scratch_shapes=[
+        scratch_shapes=WEIGHTS
+        + [
             pltpu.VMEM((chunks, C, D), BF16),
             pltpu.VMEM((chunks, C, D), BF16),
-            pltpu.VMEM(((chunks + 2) * C, D), BF16),
-            pltpu.VMEM(((chunks + 2) * C, D), BF16),
+            pltpu.VMEM((chunks * C, D), BF16),
+            pltpu.VMEM((chunks * C, D), BF16),
             pltpu.VMEM((WIN * C, C), F32),
             pltpu.VMEM((WIN, C, D), F32),
             pltpu.VMEM((WIN, C, D), F32),
             pltpu.VMEM((16, C), F32),
+            pltpu.VMEM((C, D), BF16),
             pltpu.VMEM((D, 128), BF16),
         ]
         + [pltpu.VMEM((2,) + s, t) for s, t in fetched]
         + [pltpu.VMEM((2,) + s, BF16) for s in saved]
         + [DMA((chunks,)), DMA((chunks,)), DMA((per,)), DMA((per,)), DMA((per,))]
-        + [DMA((6, 2)), DMA((4, 2)), DMA((2,))],
+        + [DMA((6, 2)), DMA((4, 2)), DMA((2,)), DMA((4,))],
         compiler_params=pltpu.CompilerParams(
             collective_id=1, has_side_effects=True, vmem_limit_bytes=VMEM_LIMIT
         ),
         name="layer_backward",
     )(
         cotangent.reshape(per, C, D),
-        doc_qr,
-        doc_kc,
+        docs,
         *weights,
         kept["x"],
         kept["q"],
@@ -612,8 +697,11 @@
 UNIT = 256
 UNITS = 9 + 3 + 12 + 12
 NARROW = 9 + 3 + 12
-X_LAG = 4
-Z_LAG = 6
+LAGS = (4, 8, 12)
+
+
+def pair_first(unit):
+    return lax.rem(unit, 4) != 3
 
 
 def dot_tn(a, b):
@@ -639,26 +727,29 @@
     right,
     act,
     made,
-    from_x,
-    from_z,
+    got_a,
+    got_b,
+    got_c,
     total,
     gain_own,
     gain_in,
     left_sems,
     right_sems,
     act_sem,
-    x_sends,
-    x_arrivals,
-    z_sends,
-    z_arrivals,
+    a_sends,
+    a_arrivals,
+    b_sends,
+    b_arrivals,
+    c_sends,
+    c_arrivals,
     out_sem,
     gain_sends,
     gain_arrivals,
 ):
     section = lax.axis_index("section")
     dp = lax.axis_index("dp")
-    x, z = lax.rem(dp, 2), dp // 2
-    partner = dp + 1 - 2 * x
+    x, near, far = lax.rem(dp, 2), lax.rem(dp // 2, 2), dp // 4
+    over_x, over_near, over_far = dp + 1 - 2 * x, dp + 2 - 4 * near, dp + 4 - 8 * far
 
     def load_left(src, slot):
         return pltpu.make_async_copy(src, left.at[slot], left_sems.at[slot])
@@ -708,26 +799,47 @@
     for step in range(1, 8):
         gain_copy(step).start()
 
-    def send_x(unit):
+    def send(unit, src, dst, sends, arrivals, to):
         pltpu.make_async_remote_copy(
-            made.at[unit, 1 - x],
-            from_x.at[unit],
-            x_sends.at[unit],
-            x_arrivals.at[unit],
-            device_id=(partner, section),
+            src,
+            dst.at[unit],
+            sends.at[unit],
+            arrivals.at[unit],
+            device_id=(to, section),
             device_id_type=MESH,
         ).start()
 
-    def send_z(unit, step):
-        target = lax.rem(z + step, 4)
-        pltpu.make_async_remote_copy(
-            made.at[unit, x, target],
-            from_z.at[unit, 3 - step],
-            z_sends.at[unit],
-            z_arrivals.at[unit],
-            device_id=(target * 2 + x, section),
-            device_id_type=MESH,
-        ).start()
+    def first_add(unit):
+        @pl.when(pair_first(unit))
+        def _():
+            send(unit, made.at[unit, 1 - x], got_a, a_sends, a_arrivals, over_x)
+
+        @pl.when(jnp.logical_not(pair_first(unit)))
+        def _():
+            send(unit, made.at[unit, :, 1 - near], got_a, a_sends, a_arrivals, over_near)
+
+    def second_add(unit):
+        await_arrival(got_a.at[unit], a_arrivals.at[unit])
+
+        @pl.when(pair_first(unit))
+        def _():
+            made[unit, x] = (made[unit, x].astype(F32) + got_a[unit].astype(F32)).astype(BF16)
+            send(unit, made.at[unit, x, 1 - near], got_b, b_sends, b_arrivals, over_near)
+
+        @pl.when(jnp.logical_not(pair_first(unit)))
+        def _():
+            made[unit, :, near] = (made[unit, :, near].astype(F32) + got_a[unit].astype(F32)).astype(BF16)
+            send(unit, made.at[unit, 1 - x, near], got_b, b_sends, b_arrivals, over_x)
+
+    def third_add(unit):
+        await_arrival(got_b.at[unit], b_arrivals.at[unit])
+        made[unit, x, near] = (made[unit, x, near].astype(F32) + got_b[unit].astype(F32)).astype(BF16)
+        send(unit, made.at[unit, x, near, 1 - far], got_c, c_sends, c_arrivals, over_far)
+
+    def finish(unit):
+        await_arrival(got_c.at[unit], c_arrivals.at[unit])
+        total[unit] = made[unit, x, near, far].astype(F32) + got_c[unit].astype(F32)
+        deliver(unit)
 
     def deliver(unit):
         for first, end, ref in ((0, 9, o_qkv), (9, 12, o_out), (12, NARROW, o_up)):
@@ -745,21 +857,11 @@
             pltpu.make_async_copy(total.at[unit], o_down.at[rows, columns], out_sem).start()
 
     def advance(now):
-        @pl.when((now >= X_LAG) & (now - X_LAG < UNITS))
-        def _():
-            unit = now - X_LAG
-            await_arrival(from_x.at[unit], x_arrivals.at[unit])
-            made[unit, x] = (made[unit, x].astype(F32) + from_x[unit].astype(F32)).astype(BF16)
-            for step in range(1, 4):
-                send_z(unit, step)
-
-        @pl.when((now >= Z_LAG) & (now - Z_LAG < UNITS))
-        def _():
-            unit = now - Z_LAG
-            await_arrival(from_z.at[unit], z_arrivals.at[unit])
-            got = from_z[unit].astype(F32)
-            total[unit] = made[unit, x, z].astype(F32) + got[0] + got[1] + got[2]
-            deliver(unit)
+        for lag, action in zip(LAGS[::-1], (finish, third_add, second_add)):
+
+            @pl.when((now >= lag) & (now - lag < UNITS))
+            def _():
+                action(now - lag)
 
     def narrow(unit, carry):
         slot = lax.rem(unit, 2)
@@ -786,8 +888,8 @@
         load_right(s_dt, 0, slot).wait()
         grad = dot_tn(left[side], right[slot]).astype(BF16)
         for shard in range(8):
-            made[unit, shard % 2, shard // 2] = grad[shard * 96 : (shard + 1) * 96]
-        send_x(unit)
+            made[unit, shard % 2, shard // 2 % 2, shard // 4] = grad[shard * 96 : (shard + 1) * 96]
+        first_add(unit)
         advance(unit)
         return carry
 
@@ -802,12 +904,12 @@
         grad = dot_tn(act[:, rows], left[1, :, columns]).astype(BF16)
         first = NARROW + 4 * column
         for part in range(4):
-            made[first + part, lax.rem(shard, 2), shard // 2] = grad[part * 96 : (part + 1) * 96]
+            made[first + part, lax.rem(shard, 2), lax.rem(shard // 2, 2), shard // 4] = grad[part * 96 : (part + 1) * 96]
 
         @pl.when(shard == 7)
         def _():
             for part in range(4):
-                send_x(first + part)
+                first_add(first + part)
 
         @pl.when(lax.rem(step, 2) == 1)
         def _():
@@ -821,7 +923,7 @@
         advance(now)
         return carry
 
-    lax.fori_loop(UNITS, UNITS + Z_LAG, drain, 0)
+    lax.fori_loop(UNITS, UNITS + LAGS[-1], drain, 0)
     for step in range(1, 8):
         gain_copy(step).wait()
     sums = gain_own[:, 0:1]
@@ -830,8 +932,9 @@
     o_gains[...] = sums
 
     def sent(unit, carry):
-        await_arrival(from_x.at[unit], x_sends.at[unit])
-        await_arrival(from_z.at[unit], z_sends.at[unit])
+        await_arrival(got_a.at[unit], a_sends.at[unit])
+        await_arrival(got_b.at[unit], b_sends.at[unit])
+        await_arrival(got_c.at[unit], c_sends.at[unit])
         return carry
 
     lax.fori_loop(0, UNITS, sent, 0)
@@ -857,15 +960,18 @@
             pltpu.VMEM((2, tokens, D), BF16),
             pltpu.VMEM((2, tokens, UNIT), BF16),
             pltpu.VMEM((tokens, FF), BF16),
-            pltpu.VMEM((UNITS, 2, 4, 96, UNIT), BF16),
-            pltpu.VMEM((UNITS, 4, 96, UNIT), BF16),
-            pltpu.VMEM((UNITS, 3, 96, UNIT), BF16),
+            pltpu.VMEM((UNITS, 2, 2, 2, 96, UNIT), BF16),
+            pltpu.VMEM((UNITS, 2, 2, 96, UNIT), BF16),
+            pltpu.VMEM((UNITS, 2, 96, UNIT), BF16),
+            pltpu.VMEM((UNITS, 96, UNIT), BF16),
             pltpu.VMEM((UNITS, 96, UNIT), F32),
             pltpu.VMEM((2, 8, D), F32),
             pltpu.VMEM((7, 2, 8, D), F32),
             DMA((2,)),
             DMA((2,)),
             DMA,
+            DMA((UNITS,)),
+            DMA((UNITS,)),
             DMA((UNITS,)),
             DMA((UNITS,)),
             DMA((UNITS,)),
@@ -881,35 +987,70 @@
     )(*operands, gains)
 
 
+def hand_over_kernel(gains, *refs):
+    sources, results, (gain_attn, gain_mlp), held = refs[:6], refs[6:12], refs[12:14], refs[14:20]
+    come, go = refs[20], refs[21]
+    arriving = [
+        pltpu.make_async_copy(src, buf, come.at[at]) for at, (src, buf) in enumerate(zip(sources, held))
+    ]
+    leaving = [
+        pltpu.make_async_copy(buf, dst, go.at[at]) for at, (buf, dst) in enumerate(zip(held, results))
+    ]
+    for copy in arriving:
+        copy.start()
+    shift = lax.rem(D - 96 * lax.axis_index("dp"), D)
+    for kind, ref in enumerate((gain_attn, gain_mlp)):
+        turned = pltpu.roll(jnp.broadcast_to(gains[kind], (8, D)), shift, 1)
+        ref[...] = turned[:1, :96]
+    for copy, onward in zip(arriving, leaving):
+        copy.wait()
+        onward.start()
+    for copy in leaving:
+        copy.wait()
+
+
+def hand_over(output, input_grad, shards, gains):
+    sds = jax.ShapeDtypeStruct
+    sources = (output, input_grad, *shards)
+    outs = pl.pallas_call(
+        hand_over_kernel,
+        out_shape=[sds(v.shape, v.dtype) for v in sources] + [sds((1, 96), F32)] * 2,
+        in_specs=[IN_VMEM] + [ANY] * 6,
+        out_specs=[ANY] * 6 + [IN_VMEM] * 2,
+        scratch_shapes=[pltpu.VMEM(v.shape, v.dtype) for v in sources] + [DMA((6,)), DMA((6,))],
+        compiler_params=pltpu.CompilerParams(vmem_limit_bytes=VMEM_LIMIT),
+        name="hand_over",
+    )(gains, *sources)
+    output, input_grad, qkv, out, up, down, gain_attn, gain_mlp = outs
+    return output, input_grad, gain_attn, qkv[None], out[None], gain_mlp, up[None], down[None]
+
+
 def body(tokens, cotangent, doc_ids, gain_attn, w_qkv, w_out, gain_mlp, w_up, w_down):
     sections = lax.axis_size("section")
     rows, seq = doc_ids.shape
     chunks = rows * seq // C
-    docs = doc_ids + 1 + 16 * jnp.arange(rows, dtype=jnp.int32)[:, None]
-    docs_q = docs.reshape(chunks, C)
-    docs_k = jnp.concatenate([jnp.zeros((2, C), jnp.int32), docs_q])
     weights = (gain_attn, gain_mlp, w_qkv[0], w_out[0], w_up[0], w_down[0])
-    output, kept = forward(sections, chunks, tokens, docs_q[:, :, None], docs_k[:, None, :], weights)
+    output, kept = forward(sections, chunks, tokens, doc_ids, weights)
     input_grad, gains, db, dh, da, dt = backward(
-        sections, chunks, cotangent, docs_q[:, None, :], docs_k[:, :, None], weights, kept
+        sections, chunks, cotangent, doc_ids, weights, kept
     )
     if lax.axis_size("dp") == 8 and chunks == 8:
         qkv, out, up, down, gains = weight_grads(
             kept["na"], dt, kept["mixed"], da, kept["nm"], dh, kept["act"], db, gains
         )
-        gains = lax.dynamic_slice(gains, (0, 0, lax.axis_index("dp") * 96), (2, 1, 96))
-        shards = (gains[0, 0], qkv, out, gains[1, 0], up, down)
-    else:
-        gains = jnp.sum(gains, axis=1)
-        grads = (
-            gains[0],
-            matmul_lt(kept["na"], dt),
-            matmul_lt(kept["mixed"], da),
-            gains[1],
-            matmul_lt(kept["nm"], dh),
-            matmul_lt(kept["act"], db),
+        return hand_over(
+            output.reshape(tokens.shape), input_grad.reshape(cotangent.shape), (qkv, out, up, down), gains
         )
-        shards = lax.psum_scatter(grads, "dp", scatter_dimension=0, tiled=True)
+    gains = jnp.sum(gains, axis=1)
+    grads = (
+        gains[0],
+        matmul_lt(kept["na"], dt),
+        matmul_lt(kept["mixed"], da),
+        gains[1],
+        matmul_lt(kept["nm"], dh),
+        matmul_lt(kept["act"], db),
+    )
+    shards = lax.psum_scatter(grads, "dp", scatter_dimension=0, tiled=True)
     return (
         output.reshape(tokens.shape),
         input_grad.reshape(cotangent.shape),

time: 459 us -> 425 us (0.926)
  Pallas kernels: 445 us -> 424 us
  local copies, waits for them, and re-layouts: 12.8 us -> 0 us
    pallas_call x1, Pallas kernels: 161 us -> 146 us  [weight_grads(): pl.pallas_call(weight_grad_kernel, out_shape=[sds((96, 3 * D), F32), sds(...]
    pallas_call x1, Pallas kernels: 93.1 us -> 85.5 us  [forward(): pl.pallas_call(functools.partial(forward_kernel, sections), out_shape=[sd...]
    unnamed x16 -> x0, local copies, waits for them, and re-layouts: 6.71 us -> none
    pallas_call x0 -> x1, Pallas kernels: none -> 5.76 us  [hand_over(): pl.pallas_call(hand_over_kernel, out_shape=[sds(v.shape, v.dtype) for v i...]
where the time goes in v3:
time: 425 us; the launch traced here: 424 us
  Pallas kernels  424 us (100%)
    pallas_call x1, Pallas kernels, backward(): pl.pallas_call(functools.partial(backward_kernel, sections), out_shape=[s...  186 us
    pallas_call x1, Pallas kernels, weight_grads(): pl.pallas_call(weight_grad_kernel, out_shape=[sds((96, 3 * D), F32), sds(...  146 us
    pallas_call x1, Pallas kernels, forward(): pl.pallas_call(functools.partial(forward_kernel, sections), out_shape=[sd...  85.5 us

profile of v3, /device:TPU:0, one launch (start us, length us, event | category | flops | bytes accessed | tf_op | source)
XLA Modules:
  0.0 424.4 jit_solution(1470454581403911683)
XLA Ops:
  0.6 85.5 %layer_forward.1 = (bf16[2,256,768]{2,1,0:T(8,128)(2,1)}, bf16[8,256,768]{2,1,0:T(8,128)(2,1)}, bf16[8,256,768]{2,1,0:T(8,128)(2,1)}, bf16[8,256,768]{2,1,0:T(8,...) custom-call(bf16[2,256,768]{2,1,0:T(8,128)(2,1)} %bitcast.40, ...), custom_call_target="tpu_custom_call" | custom-call | tf_op jit(solution)/shard_map/layer_forward/pallas_call | solution.py:610
  86.1 186.1 %layer_backward.1 = (bf16[2,256,768]{2,1,0:T(8,128)(2,1)}, f32[2,8,768]{2,1,0:T(8,128)}, bf16[8,256,768]{2,1,0:T(8,128)(2,1)}, bf16[8,256,3072]{2,1,0:T(8,128)(2...) custom-call(bf16[2,256,768]{2,1,0:T(8,128)(2,1)} %bitcast.43, s32[2,1024]{1,0:T(2,128)} %docs.3, ...), custom_call_target="tpu_custom_call" | custom-call | tf_op jit(solution)/shard_map/layer_backward/pallas_call | solution.py:645
  272.2 146.3 %weight_grads.1 = (f32[96,2304]{1,0:T(8,128)}, f32[96,768]{1,0:T(8,128)}, f32[96,3072]{1,0:T(8,128)}, f32[384,768]{1,0:T(8,128)}, f32[2,1,768]{2,1,0:T(1,128)}) custom-call(bf16[2048,768]{1,0:T(8,128)(2,1)} %bitcast.34, bf16[2048,2304]{1,0:T(8,128)(2,1)} %bitcast.31, bf16[2048,768]{1,0:T(8,128)(2,1)} %bitcast.28, bf16[2048,768]{1,0:T(8,128)(2,1)} %bitcast.37, ...), custom_call_target="tpu_custom_call" | custom-call | tf_op jit(solution)/shard_map/weight_grads/pallas_call | solution.py:948
  418.5 5.8 %hand_over.1 = (bf16[512,768]{1,0:T(8,128)(2,1)}, bf16[512,768]{1,0:T(8,128)(2,1)}, f32[96,2304]{1,0:T(8,128)}, f32[96,768]{1,0:T(8,128)}, f32[96,3072]{1,0:T(8,...) custom-call(f32[2,1,768]{2,1,0:T(1,128)} %get-tuple-element.55.gains, bf16[512,768]{1,0:T(8,128)(2,1)} %bitcast.41, ...), custom_call_target="tpu_custom_call" | custom-call | tf_op jit(solution)/shard_map/hand_over/pallas_call | solution.py:1015

commit v4 on v3

--- a/solution.py
+++ b/solution.py
@@ -86,14 +86,14 @@
             pltpu.make_async_copy(rows.at[piece], rows.at[piece], send_sems.at[piece]).wait()
 
 
-def pass_on(section, chunk, per, last, step, outbox, inbox, result, sends, arrivals, landed, kept):
+def pass_on(section, chunk, per, last, step, source, inbox, result, sends, arrivals, landed):
     dp = lax.axis_index("dp")
     owner = chunk // per
 
     @pl.when(section != last)
     def _():
         pltpu.make_async_remote_copy(
-            outbox.at[chunk],
+            source,
             inbox.at[chunk],
             sends.at[chunk],
             arrivals.at[chunk],
@@ -104,7 +104,7 @@
     @pl.when((section == last) & (owner != last))
     def _():
         pltpu.make_async_remote_copy(
-            outbox.at[chunk],
+            source,
             result.at[lax.rem(chunk, per)],
             sends.at[chunk],
             landed.at[lax.rem(chunk, per)],
@@ -114,29 +114,20 @@
 
     @pl.when((section == last) & (owner == last))
     def _():
-        pltpu.make_async_copy(
-            outbox.at[chunk], result.at[lax.rem(chunk, per)], kept.at[lax.rem(chunk, per)]
-        ).start()
-
-
-def settle(section, chunks, per, last, outbox, result, sends, landed, kept):
+        pltpu.make_async_copy(source, result.at[lax.rem(chunk, per)], sends.at[chunk]).start()
+
+
+def settle(section, first, end, per, last, source, result, sends, landed):
     def one(chunk, carry):
-        @pl.when((section != last) | (chunk // per != last))
-        def _():
-            await_arrival(outbox.at[chunk], sends.at[chunk])
-
+        await_arrival(source, sends.at[chunk])
         return carry
 
-    lax.fori_loop(0, chunks, one, 0)
+    lax.fori_loop(first, end, one, 0)
     for piece in range(per):
 
         @pl.when(section != last)
         def _():
             await_arrival(result.at[piece], landed.at[piece])
-
-        @pl.when(section == last)
-        def _():
-            await_arrival(result.at[piece], kept.at[piece])
 
 
 def fill_bias(docs, chunk, bias, keys_down):
@@ -180,9 +171,10 @@
             attend(blocks)
 
 
-def forward_kernel(
+def layer_kernel(
     sections,
     tokens,
+    cotangent,
     docs,
     gain_a,
     gain_m,
@@ -191,10 +183,9 @@
     h_up,
     h_down,
     result,
-    s_x,
+    grad_result,
+    gains,
     s_q,
-    s_k,
-    s_v,
     s_na,
     s_mixed,
     s_lse,
@@ -202,15 +193,26 @@
     s_nm,
     s_act,
     s_dg,
+    s_db,
+    s_dh,
+    s_da,
+    s_dt,
     w_qkv,
     w_out,
     w_up,
     w_down,
     inbox,
     outbox,
+    grads,
     kbuf,
     vbuf,
-    bias,
+    bias_f,
+    bias_b,
+    dk_acc,
+    dv_acc,
+    lse_d,
+    b_dmix,
+    marks,
     b_q,
     b_na,
     b_mixed,
@@ -219,17 +221,24 @@
     b_nm,
     b_act,
     b_dg,
+    b_dt,
     arrivals,
     sends,
     first_sends,
     landed,
-    kept,
-    saves,
+    grad_arrivals,
+    grad_sends,
+    grad_first_sends,
+    grad_landed,
+    kept_f,
+    kept_b,
+    loads,
     weight_sems,
 ):
     section = lax.axis_index("section")
     chunks = inbox.shape[0]
     per = tokens.shape[0]
+    last = sections - 1
     weights = [
         pltpu.make_async_copy(src, dst, weight_sems.at[kind])
         for kind, (src, dst) in enumerate(
@@ -244,56 +253,62 @@
         def _():
             copy.wait()
 
+    def clear():
+        dk_acc[...] = jnp.zeros_like(dk_acc)
+        dv_acc[...] = jnp.zeros_like(dv_acc)
+        gains[...] = jnp.zeros_like(gains)
+        owner_of = lax.broadcasted_iota(jnp.int32, (D, 128), 0) // HD
+        own = owner_of == lax.broadcasted_iota(jnp.int32, (D, 128), 1)
+        marks[...] = own.astype(F32).astype(BF16)
+
     greet(section, sections)
     scatter_rows(section, sections, per, tokens, inbox, arrivals, first_sends, 0)
+    scatter_rows(section, sections, per, cotangent, grads, grad_arrivals, grad_first_sends, last)
     low, high, is_low = lane_masks()
     centered = jnp.where(section == 0, 1.0, 0.0).astype(F32)
 
-    def stores(chunk, slot):
-        here = pl.ds(pl.multiple_of(chunk * C, C), C)
+    @pl.when(section != 0)
+    def _():
+        clear()
+
+    def keep_forward(chunk, slot):
         pairs = (
-            (inbox.at[chunk], s_x),
-            (kbuf.at[here], s_k),
-            (vbuf.at[here], s_v),
-            (b_q.at[slot], s_q),
-            (b_na.at[slot], s_na),
-            (b_mixed.at[slot], s_mixed),
-            (b_lse.at[slot], s_lse),
-            (b_mid.at[slot], s_mid),
-            (b_nm.at[slot], s_nm),
-            (b_act.at[slot], s_act),
-            (b_dg.at[slot], s_dg),
+            (b_q, s_q),
+            (b_na, s_na),
+            (b_mixed, s_mixed),
+            (b_lse, s_lse),
+            (b_mid, s_mid),
+            (b_nm, s_nm),
+            (b_act, s_act),
+            (b_dg, s_dg),
         )
         return [
-            pltpu.make_async_copy(src, dst.at[chunk], saves.at[kind, slot])
+            pltpu.make_async_copy(src.at[slot], dst.at[chunk], kept_f.at[kind, slot])
             for kind, (src, dst) in enumerate(pairs)
         ]
 
-    def one_chunk(chunk, carry):
+    def forward_chunk(chunk, carry):
         slot = lax.rem(chunk, 2)
 
         @pl.when(chunk >= 2)
         def _():
-            for copy in stores(chunk - 2, slot):
+            for copy in keep_forward(chunk - 2, slot):
                 copy.wait()
 
-        todo = stores(chunk, slot)
+        todo = keep_forward(chunk, slot)
         at_first(chunk, weights[0])
-        fill_bias(docs, chunk, bias, False)
+        fill_bias(docs, chunk, bias_f, False)
         await_arrival(inbox.at[chunk], arrivals.at[chunk])
-        todo[0].start()
         x = inbox[chunk].astype(F32)
         x = x - centered * row_mean(x)
         na = (x * lax.rsqrt(row_mean(x * x) + EPS) * gain_a[...]).astype(BF16)
         b_na[slot] = na
-        todo[4].start()
+        todo[1].start()
         b_q[slot] = (dot(na, w_qkv[:, :D]).astype(BF16) * (HD**-0.5)).astype(BF16)
         here = pl.ds(pl.multiple_of(chunk * C, C), C)
         kbuf[here, :] = dot(na, w_qkv[:, D : 2 * D]).astype(BF16)
         vbuf[here, :] = dot(na, w_qkv[:, 2 * D :]).astype(BF16)
-        todo[1].start()
-        todo[2].start()
-        todo[3].start()
+        todo[0].start()
         lane = lax.broadcasted_iota(jnp.int32, (1, 128), 1)
 
         def attend(blocks):
@@ -303,7 +318,7 @@
             for pair in range(PAIRS):
                 lanes = slice(pair * 2 * HD, (pair + 1) * 2 * HD)
                 q2 = two_heads(b_q[slot, :, lanes], low, high)
-                s = dot_nt(q2, kbuf[window, lanes]).reshape(2, C, blocks * C) + bias[:, masked][None]
+                s = dot_nt(q2, kbuf[window, lanes]).reshape(2, C, blocks * C) + bias_f[:, masked][None]
                 top = jnp.max(s, axis=-1, keepdims=True)
                 e = jnp.exp(s - top)
                 total = jnp.sum(e, axis=-1, keepdims=True)
@@ -316,16 +331,16 @@
             b_lse[slot] = jnp.transpose(lse_all)[:16]
 
         by_blocks(docs, chunk, attend)
-        todo[5].start()
-        todo[6].start()
+        todo[2].start()
+        todo[3].start()
         at_first(chunk, weights[1])
         branch = dot(b_mixed[slot], w_out[...])
         mid = x + branch - row_mean(branch)
         b_mid[slot] = mid
-        todo[7].start()
+        todo[4].start()
         nm = (mid * lax.rsqrt(row_mean(mid * mid) + EPS) * gain_m[...]).astype(BF16)
         b_nm[slot] = nm
-        todo[8].start()
+        todo[5].start()
         at_first(chunk, weights[2])
         k0 = 0.7978845608028654
         k1 = 0.044715
@@ -338,174 +353,77 @@
             b_act[slot, :, cols] = (h * half).astype(BF16)
             slope = half + (h * (1.0 - t * t)) * (0.5 * k0 + (1.5 * k0 * k1) * h2)
             b_dg[slot, :, cols] = slope.astype(BF16)
-        todo[9].start()
-        todo[10].start()
+        todo[6].start()
+        todo[7].start()
         at_first(chunk, weights[3])
         branch = dot(b_act[slot], w_down[...])
-        outbox[chunk] = (b_mid[slot] + branch - row_mean(branch)).astype(BF16)
-        pass_on(section, chunk, per, sections - 1, 1, outbox, inbox, result, sends, arrivals, landed, kept)
+
+        @pl.when(chunk >= 2)
+        def _():
+            await_arrival(outbox.at[slot], sends.at[chunk - 2])
+
+        outbox[slot] = (b_mid[slot] + branch - row_mean(branch)).astype(BF16)
+        pass_on(section, chunk, per, last, 1, outbox.at[slot], inbox, result, sends, arrivals, landed)
         return carry
 
-    lax.fori_loop(0, chunks, one_chunk, 0)
+    lax.fori_loop(0, chunks, forward_chunk, 0)
     for chunk in (chunks - 2, chunks - 1):
-        for copy in stores(chunk, chunk % 2):
+        for copy in keep_forward(chunk, chunk % 2):
             copy.wait()
-    drain_rows(section, sections, per, tokens, first_sends, 0)
-    settle(section, chunks, per, sections - 1, outbox, result, sends, landed, kept)
-
-
-def backward_kernel(
-    sections,
-    cotangent,
-    docs,
-    gain_a,
-    gain_m,
-    h_qkv,
-    h_out,
-    h_up,
-    h_down,
-    s_x,
-    s_q,
-    s_k,
-    s_v,
-    s_mixed,
-    s_lse,
-    s_mid,
-    s_dg,
-    result,
-    gains,
-    s_db,
-    s_dh,
-    s_da,
-    s_dt,
-    w_qkv,
-    w_out,
-    w_up,
-    w_down,
-    inbox,
-    outbox,
-    kbuf,
-    vbuf,
-    bias,
-    dk_acc,
-    dv_acc,
-    lse_d,
-    b_dmix,
-    marks,
-    b_x,
-    b_q,
-    b_mixed,
-    b_lse,
-    b_mid,
-    b_dg,
-    b_db,
-    b_dh,
-    b_da,
-    b_dt,
-    arrivals,
-    sends,
-    first_sends,
-    landed,
-    kept,
-    loads,
-    saves,
-    kv_sems,
-    weight_sems,
-):
-    section = lax.axis_index("section")
-    chunks = inbox.shape[0]
-    per = cotangent.shape[0]
-    last = sections - 1
+
+    @pl.when(section == 0)
+    def _():
+        clear()
 
     def fetches(chunk, slot):
-        pairs = (
-            (s_dg, b_dg),
-            (s_mid, b_mid),
-            (s_mixed, b_mixed),
-            (s_q, b_q),
-            (s_lse, b_lse),
-            (s_x, b_x),
-        )
+        pairs = ((s_dg, b_dg), (s_mid, b_mid), (s_mixed, b_mixed), (s_q, b_q), (s_lse, b_lse))
         return [
             pltpu.make_async_copy(src.at[chunk], dst.at[slot], loads.at[kind, slot])
             for kind, (src, dst) in enumerate(pairs)
         ]
 
-    def stores(chunk, slot):
-        pairs = ((b_db, s_db), (b_dh, s_dh), (b_da, s_da), (b_dt, s_dt))
+    def keep_backward(chunk, slot):
+        pairs = ((b_nm, s_db), (b_act, s_dh), (b_na, s_da), (b_dt, s_dt))
         return [
-            pltpu.make_async_copy(src.at[slot], dst.at[chunk], saves.at[kind, slot])
+            pltpu.make_async_copy(src.at[slot], dst.at[chunk], kept_b.at[kind, slot])
             for kind, (src, dst) in enumerate(pairs)
         ]
 
-    kv_copies = [
-        pltpu.make_async_copy(s_k, kbuf, kv_sems.at[0]),
-        pltpu.make_async_copy(s_v, vbuf, kv_sems.at[1]),
-    ]
-    weights = [
-        pltpu.make_async_copy(src, dst, weight_sems.at[kind])
-        for kind, (src, dst) in enumerate(
-            ((h_down, w_down), (h_up, w_up), (h_out, w_out), (h_qkv, w_qkv))
-        )
-    ]
-    weights[0].start()
-    for copy in fetches(chunks - 1, 0):
-        copy.start()
-    weights[1].start()
-    weights[2].start()
-    for copy in kv_copies:
-        copy.start()
-    weights[3].start()
-
-    def at_first(step, copy):
-        @pl.when(step == 0)
-        def _():
-            copy.wait()
-
-    greet(section, sections)
-    scatter_rows(section, sections, per, cotangent, inbox, arrivals, first_sends, last)
-    low, high, _ = lane_masks()
-    dk_acc[...] = jnp.zeros_like(dk_acc)
-    dv_acc[...] = jnp.zeros_like(dv_acc)
-    gains[...] = jnp.zeros_like(gains)
-    owner_of = lax.broadcasted_iota(jnp.int32, (D, 128), 0) // HD
-    marks[...] = (owner_of == lax.broadcasted_iota(jnp.int32, (D, 128), 1)).astype(F32).astype(BF16)
-    centered = jnp.where(section == 0, 1.0, 0.0).astype(F32)
-
     def folded(v):
         return jnp.sum(v.reshape(C // 8, 8, D), axis=0)
 
-    def one_chunk(step, carry):
+    def backward_chunk(step, carry):
         chunk = chunks - 1 - step
-        slot = lax.rem(step, 2)
-
-        @pl.when(step + 1 < chunks)
+        slot = lax.rem(chunk, 2)
+
+        @pl.when((step >= 1) & (chunk >= 1))
         def _():
             for copy in fetches(chunk - 1, 1 - slot):
                 copy.start()
 
         @pl.when(step >= 2)
         def _():
-            for copy in stores(chunk + 2, slot):
+            for copy in keep_backward(chunk + 2, slot):
                 copy.wait()
 
-        for copy in fetches(chunk, slot):
-            copy.wait()
-        todo = stores(chunk, slot)
-        at_first(step, weights[0])
-        fill_bias(docs, chunk, bias, True)
-        await_arrival(inbox.at[chunk], arrivals.at[chunk])
-        g = inbox[chunk].astype(F32)
+        @pl.when(step >= 2)
+        def _():
+            for copy in fetches(chunk, slot):
+                copy.wait()
+
+        todo = keep_backward(chunk, slot)
+        fill_bias(docs, chunk, bias_b, True)
+        await_arrival(grads.at[chunk], grad_arrivals.at[chunk])
+        g = grads[chunk].astype(F32)
         db = (g - row_mean(g)).astype(BF16)
-        b_db[slot] = db
+        b_nm[slot] = db
         todo[0].start()
         for part in range(FF // D):
             cols = slice(part * D, (part + 1) * D)
             d_active = dot_nt(db, w_down[cols, :])
-            b_dh[slot, :, cols] = (d_active * b_dg[slot, :, cols].astype(F32)).astype(BF16)
+            b_act[slot, :, cols] = (d_active * b_dg[slot, :, cols].astype(F32)).astype(BF16)
         todo[1].start()
-        at_first(step, weights[1])
-        dn = dot_nt(b_dh[slot], w_up[...])
+        dn = dot_nt(b_act[slot], w_up[...])
         mid = b_mid[slot]
         factor = lax.rsqrt(row_mean(mid * mid) + EPS)
         unit = mid * factor
@@ -513,10 +431,9 @@
         dn = dn * gain_m[...]
         d_mid = g + factor * (dn - unit * row_mean(dn * unit))
         da = (d_mid - row_mean(d_mid)).astype(BF16)
-        b_da[slot] = da
+        b_na[slot] = da
         todo[2].start()
         b_mid[slot] = d_mid
-        at_first(step, weights[2])
         dmix = dot_nt(da, w_out[...]).astype(BF16)
         b_dmix[...] = dmix
         prod = dmix.astype(F32) * b_mixed[slot].astype(F32)
@@ -524,9 +441,6 @@
         rest = (prod - top.astype(F32)).astype(BF16)
         inner = dot(top, marks[...]) + dot(rest, marks[...])
         lse_d[...] = jnp.transpose(inner)[:16]
-        for copy in kv_copies:
-            at_first(step, copy)
-
         def attend(blocks):
             window = pl.ds(pl.multiple_of((chunk - blocks + 1) * C, C), blocks * C)
             masked = slice((WIN - blocks) * C, WIN * C)
@@ -536,7 +450,7 @@
                 do2 = two_heads(b_dmix[:, lanes], low, high)
                 keys = kbuf[window, lanes]
                 values = vbuf[window, lanes]
-                both = jnp.concatenate([bias[masked, :], bias[masked, :]], axis=1)
+                both = jnp.concatenate([bias_b[masked, :], bias_b[masked, :]], axis=1)
                 even, odd = slice(2 * pair, 2 * pair + 1), slice(2 * pair + 1, 2 * pair + 2)
                 lse = jnp.concatenate([b_lse[slot, even, :], b_lse[slot, odd, :]], axis=1)
                 inner = jnp.concatenate([lse_d[even, :], lse_d[odd, :]], axis=1)
@@ -560,9 +474,8 @@
         dk_acc[done] = jnp.zeros((C, D), F32)
         dv_acc[done] = jnp.zeros((C, D), F32)
         todo[3].start()
-        at_first(step, weights[3])
         dn = dot_nt(b_dt[slot], w_qkv[...])
-        x = b_x[slot].astype(F32)
+        x = inbox[chunk].astype(F32)
         x = x - centered * row_mean(x)
         factor = lax.rsqrt(row_mean(x * x) + EPS)
         unit = x * factor
@@ -570,16 +483,20 @@
         dn = dn * gain_a[...]
         grad = b_mid[slot] + factor * (dn - unit * row_mean(dn * unit))
         grad = grad - centered * row_mean(grad)
-        outbox[chunk] = grad.astype(BF16)
-        pass_on(section, chunk, per, 0, -1, outbox, inbox, result, sends, arrivals, landed, kept)
+        inbox[chunk] = grad.astype(BF16)
+        pass_on(
+            section, chunk, per, 0, -1, inbox.at[chunk], grads, grad_result, grad_sends, grad_arrivals, grad_landed
+        )
         return carry
 
-    lax.fori_loop(0, chunks, one_chunk, 0)
-    for step in (chunks - 2, chunks - 1):
-        for copy in stores(chunks - 1 - step, step % 2):
+    lax.fori_loop(0, chunks, backward_chunk, 0)
+    for chunk in (0, 1):
+        for copy in keep_backward(chunk, chunk):
             copy.wait()
-    drain_rows(section, sections, per, cotangent, first_sends, last)
-    settle(section, chunks, per, 0, outbox, result, sends, landed, kept)
+    drain_rows(section, sections, per, tokens, first_sends, 0)
+    drain_rows(section, sections, per, cotangent, grad_first_sends, last)
+    settle(section, chunks - 2, chunks, per, last, outbox.at[0], result, sends, landed)
+    settle(section, 0, chunks, per, 0, inbox.at[0], grad_result, grad_sends, grad_landed)
 
 
 ANY = pl.BlockSpec(memory_space=pl.ANY)
@@ -587,17 +504,11 @@
 DMA = pltpu.SemaphoreType.DMA
 
 
-WEIGHTS = [pltpu.VMEM(shape, BF16) for shape in ((D, 3 * D), (D, D), (D, FF), (FF, D))]
-
-
-def forward(sections, chunks, tokens, docs, weights):
+def layers(sections, chunks, tokens, cotangent, docs, weights):
     per = chunks // sections
     sds = jax.ShapeDtypeStruct
-    saved = (
-        ("x", (C, D), BF16),
+    staged = (
         ("q", (C, D), BF16),
-        ("k", (C, D), BF16),
-        ("v", (C, D), BF16),
         ("na", (C, D), BF16),
         ("mixed", (C, D), BF16),
         ("lse", (16, C), F32),
@@ -606,53 +517,27 @@
         ("act", (C, FF), BF16),
         ("dg", (C, FF), BF16),
     )
-    staged = [entry for entry in saved if entry[0] not in ("x", "k", "v")]
+    saved = staged + (
+        ("db", (C, D), BF16),
+        ("dh", (C, FF), BF16),
+        ("da", (C, D), BF16),
+        ("dt", (C, 3 * D), BF16),
+    )
     outs = pl.pallas_call(
-        functools.partial(forward_kernel, sections),
-        out_shape=[sds((per, C, D), BF16)] + [sds((chunks,) + s, t) for _, s, t in saved],
-        in_specs=[ANY] + [IN_VMEM] * 3 + [ANY] * 4,
-        out_specs=[ANY] * (1 + len(saved)),
-        scratch_shapes=WEIGHTS
+        functools.partial(layer_kernel, sections),
+        out_shape=[sds((per, C, D), BF16)] * 2
+        + [sds((2, 8, D), F32)]
+        + [sds((chunks,) + s, t) for _, s, t in saved],
+        in_specs=[ANY] * 2 + [IN_VMEM] * 3 + [ANY] * 4,
+        out_specs=[ANY] * 2 + [IN_VMEM] + [ANY] * len(saved),
+        scratch_shapes=[pltpu.VMEM(shape, BF16) for shape in ((D, 3 * D), (D, D), (D, FF), (FF, D))]
         + [
             pltpu.VMEM((chunks, C, D), BF16),
+            pltpu.VMEM((2, C, D), BF16),
             pltpu.VMEM((chunks, C, D), BF16),
             pltpu.VMEM((chunks * C, D), BF16),
             pltpu.VMEM((chunks * C, D), BF16),
             pltpu.VMEM((C, WIN * C), F32),
-        ]
-        + [pltpu.VMEM((2,) + s, t) for _, s, t in staged]
-        + [DMA((chunks,)), DMA((chunks,)), DMA((per,)), DMA((per,)), DMA((per,)), DMA((11, 2)), DMA((4,))],
-        compiler_params=pltpu.CompilerParams(
-            collective_id=0, has_side_effects=True, vmem_limit_bytes=VMEM_LIMIT
-        ),
-        name="layer_forward",
-    )(tokens.reshape(per, C, D), docs, *weights)
-    return outs[0], {name: out for (name, _, _), out in zip(saved, outs[1:])}
-
-
-def backward(sections, chunks, cotangent, docs, weights, kept):
-    per = chunks // sections
-    sds = jax.ShapeDtypeStruct
-    fetched = (
-        ((C, D), BF16),
-        ((C, D), BF16),
-        ((C, D), BF16),
-        ((16, C), F32),
-        ((C, D), F32),
-        ((C, FF), BF16),
-    )
-    saved = ((C, D), (C, FF), (C, D), (C, 3 * D))
-    outs = pl.pallas_call(
-        functools.partial(backward_kernel, sections),
-        out_shape=[sds((per, C, D), BF16), sds((2, 8, D), F32)] + [sds((chunks,) + s, BF16) for s in saved],
-        in_specs=[ANY] + [IN_VMEM] * 3 + [ANY] * 12,
-        out_specs=[ANY, IN_VMEM] + [ANY] * len(saved),
-        scratch_shapes=WEIGHTS
-        + [
-            pltpu.VMEM((chunks, C, D), BF16),
-            pltpu.VMEM((chunks, C, D), BF16),
-            pltpu.VMEM((chunks * C, D), BF16),
-            pltpu.VMEM((chunks * C, D), BF16),
             pltpu.VMEM((WIN * C, C), F32),
             pltpu.VMEM((WIN, C, D), F32),
             pltpu.VMEM((WIN, C, D), F32),
@@ -660,28 +545,16 @@
             pltpu.VMEM((C, D), BF16),
             pltpu.VMEM((D, 128), BF16),
         ]
-        + [pltpu.VMEM((2,) + s, t) for s, t in fetched]
-        + [pltpu.VMEM((2,) + s, BF16) for s in saved]
-        + [DMA((chunks,)), DMA((chunks,)), DMA((per,)), DMA((per,)), DMA((per,))]
-        + [DMA((6, 2)), DMA((4, 2)), DMA((2,)), DMA((4,))],
+        + [pltpu.VMEM((2,) + s, t) for _, s, t in staged]
+        + [pltpu.VMEM((2, C, 3 * D), BF16)]
+        + [DMA((chunks,)), DMA((chunks,)), DMA((per,)), DMA((per,))] * 2
+        + [DMA((8, 2)), DMA((4, 2)), DMA((5, 2)), DMA((4,))],
         compiler_params=pltpu.CompilerParams(
-            collective_id=1, has_side_effects=True, vmem_limit_bytes=VMEM_LIMIT
+            collective_id=0, has_side_effects=True, vmem_limit_bytes=VMEM_LIMIT
         ),
-        name="layer_backward",
-    )(
-        cotangent.reshape(per, C, D),
-        docs,
-        *weights,
-        kept["x"],
-        kept["q"],
-        kept["k"].reshape(chunks * C, D),
-        kept["v"].reshape(chunks * C, D),
-        kept["mixed"],
-        kept["lse"],
-        kept["mid"],
-        kept["dg"],
-    )
-    return outs
+        name="layers",
+    )(tokens.reshape(per, C, D), cotangent.reshape(per, C, D), docs, *weights)
+    return outs[0], outs[1], outs[2], {name: out for (name, _, _), out in zip(saved, outs[3:])}
 
 
 def matmul_lt(left_side, right_side):
@@ -1030,10 +903,8 @@
     rows, seq = doc_ids.shape
     chunks = rows * seq // C
     weights = (gain_attn, gain_mlp, w_qkv[0], w_out[0], w_up[0], w_down[0])
-    output, kept = forward(sections, chunks, tokens, doc_ids, weights)
-    input_grad, gains, db, dh, da, dt = backward(
-        sections, chunks, cotangent, doc_ids, weights, kept
-    )
+    output, input_grad, gains, kept = layers(sections, chunks, tokens, cotangent, doc_ids, weights)
+    db, dh, da, dt = kept["db"], kept["dh"], kept["da"], kept["dt"]
     if lax.axis_size("dp") == 8 and chunks == 8:
         qkv, out, up, down, gains = weight_grads(
             kept["na"], dt, kept["mixed"], da, kept["nm"], dh, kept["act"], db, gains

time: 425 us -> 412 us (0.969)
  Pallas kernels: 424 us -> 411 us
    pallas_call x2 -> x1, Pallas kernels: 272 us -> 259 us  [layers(): pl.pallas_call(functools.partial(layer_kernel, sections), out_shape=[sds(...]
where the time goes in v4:
time: 412 us
  Pallas kernels  411 us (100%)
    pallas_call x1, Pallas kernels, layers(): pl.pallas_call(functools.partial(layer_kernel, sections), out_shape=[sds(...  259 us
    pallas_call x1, Pallas kernels, weight_grads(): pl.pallas_call(weight_grad_kernel, out_shape=[sds((96, 3 * D), F32), sds(...  146 us

profile of v4, /device:TPU:0, one launch (start us, length us, event | category | flops | bytes accessed | tf_op | source)
XLA Modules:
  0.0 411.7 jit_solution(7044841261679091649)
XLA Ops:
  0.6 258.7 %layers.1 = (bf16[2,256,768]{2,1,0:T(8,128)(2,1)}, bf16[2,256,768]{2,1,0:T(8,128)(2,1)}, f32[2,8,768]{2,1,0:T(8,128)}, bf16[8,256,768]{2,1,0:T(8,128)(2,1)}, bf1...) custom-call(bf16[2,256,768]{2,1,0:T(8,128)(2,1)} %bitcast.32, ...), custom_call_target="tpu_custom_call" | custom-call | tf_op jit(solution)/shard_map/layers/pallas_call | solution.py:526
  259.3 146.4 %weight_grads.1 = (f32[96,2304]{1,0:T(8,128)}, f32[96,768]{1,0:T(8,128)}, f32[96,3072]{1,0:T(8,128)}, f32[384,768]{1,0:T(8,128)}, f32[2,1,768]{2,1,0:T(1,128)}) custom-call(bf16[2048,768]{1,0:T(8,128)(2,1)} %bitcast.26, bf16[2048,2304]{1,0:T(8,128)(2,1)} %bitcast.22, bf16[2048,768]{1,0:T(8,128)(2,1)} %bitcast.27, bf16[2048,768]{1,0:T(8,128)(2,1)} %bitcast.30, ...), custom_call_target="tpu_custom_call" | custom-call | tf_op jit(solution)/shard_map/weight_grads/pallas_call | solution.py:821
  405.7 5.8 %hand_over.1 = (bf16[512,768]{1,0:T(8,128)(2,1)}, bf16[512,768]{1,0:T(8,128)(2,1)}, f32[96,2304]{1,0:T(8,128)}, f32[96,768]{1,0:T(8,128)}, f32[96,3072]{1,0:T(8,...) custom-call(f32[2,1,768]{2,1,0:T(1,128)} %get-tuple-element.41.gains, bf16[512,768]{1,0:T(8,128)(2,1)} %bitcast.34, ...), custom_call_target="tpu_custom_call" | custom-call | tf_op jit(solution)/shard_map/hand_over/pallas_call | solution.py:888

commit v5 on v4

--- a/solution.py
+++ b/solution.py
@@ -570,6 +570,8 @@
 UNIT = 256
 UNITS = 9 + 3 + 12 + 12
 NARROW = 9 + 3 + 12
+LENT = 6
+LENT_SHORT = 3
 LAGS = (4, 8, 12)
 
 
@@ -618,10 +620,22 @@
     out_sem,
     gain_sends,
     gain_arrivals,
+    lent_sends,
+    lent_arrivals,
+    back_sends,
+    back_arrivals,
+    here,
 ):
     section = lax.axis_index("section")
     dp = lax.axis_index("dp")
     x, near, far = lax.rem(dp, 2), lax.rem(dp // 2, 2), dp // 4
+    lender = section < 2
+    across = 3 - section
+    loan = jnp.where((section == 0) | (section == 3), LENT, LENT_SHORT)
+
+    def lent(unit):
+        return (unit < 2 * loan) & (lax.rem(unit, 2) == 1)
+
     over_x, over_near, over_far = dp + 1 - 2 * x, dp + 2 - 4 * near, dp + 4 - 8 * far
 
     def load_left(src, slot):
@@ -656,7 +670,16 @@
     for step in range(1, 8):
         other = lax.rem(dp + step, 8)
         pl.semaphore_signal(barrier, inc=1, device_id=(other, section), device_id_type=MESH)
-    pl.semaphore_wait(barrier, 7)
+
+    @pl.when(lender)
+    def _():
+        pl.semaphore_wait(barrier, 8)
+        pl.semaphore_signal(here, inc=1, device_id=(dp, across), device_id_type=MESH)
+
+    @pl.when(jnp.logical_not(lender))
+    def _():
+        pl.semaphore_signal(barrier, inc=1, device_id=(dp, across), device_id_type=MESH)
+        pl.semaphore_wait(barrier, 7)
 
     def gain_copy(step):
         other = lax.rem(dp + step, 8)
@@ -712,7 +735,38 @@
     def finish(unit):
         await_arrival(got_c.at[unit], c_arrivals.at[unit])
         total[unit] = made[unit, x, near, far].astype(F32) + got_c[unit].astype(F32)
-        deliver(unit)
+
+        @pl.when(unit < UNITS)
+        def _():
+            deliver(unit)
+
+        @pl.when(unit >= UNITS)
+        def _():
+            give_back(unit - UNITS)
+
+    def lend(place):
+        pltpu.make_async_remote_copy(
+            made.at[2 * place + 1],
+            made.at[UNITS + place],
+            lent_sends.at[place],
+            lent_arrivals.at[place],
+            device_id=(dp, across),
+            device_id_type=MESH,
+        ).start()
+
+    def give_back(place):
+        pltpu.make_async_remote_copy(
+            total.at[UNITS + place],
+            total.at[2 * place + 1],
+            back_sends.at[place],
+            back_arrivals.at[place],
+            device_id=(dp, across),
+            device_id_type=MESH,
+        ).start()
+
+    def added_here(unit):
+        kept = lender & (unit < UNITS) & jnp.logical_not(lent(unit))
+        return kept | (jnp.logical_not(lender) & (unit < UNITS + loan))
 
     def deliver(unit):
         for first, end, ref in ((0, 9, o_qkv), (9, 12, o_out), (12, NARROW, o_up)):
@@ -732,7 +786,7 @@
     def advance(now):
         for lag, action in zip(LAGS[::-1], (finish, third_add, second_add)):
 
-            @pl.when((now >= lag) & (now - lag < UNITS))
+            @pl.when((now >= lag) & added_here(now - lag))
             def _():
                 action(now - lag)
 
@@ -762,7 +816,15 @@
         grad = dot_tn(left[side], right[slot]).astype(BF16)
         for shard in range(8):
             made[unit, shard % 2, shard // 2 % 2, shard // 4] = grad[shard * 96 : (shard + 1) * 96]
-        first_add(unit)
+
+        @pl.when(lender & lent(unit))
+        def _():
+            lend(lax.rem(unit, 2 * LENT) // 2)
+
+        @pl.when(added_here(unit))
+        def _():
+            first_add(unit)
+
         advance(unit)
         return carry
 
@@ -796,7 +858,23 @@
         advance(now)
         return carry
 
-    lax.fori_loop(UNITS, UNITS + LAGS[-1], drain, 0)
+    @pl.when(jnp.logical_not(lender))
+    def _():
+        pl.semaphore_wait(here, 1)
+
+        def borrowed(unit, carry):
+            await_arrival(made.at[unit], lent_arrivals.at[unit - UNITS])
+            first_add(unit)
+            advance(unit)
+            return carry
+
+        lax.fori_loop(UNITS, UNITS + loan, borrowed, 0)
+        lax.fori_loop(UNITS + loan, UNITS + loan + LAGS[-1], drain, 0)
+
+    @pl.when(lender)
+    def _():
+        lax.fori_loop(UNITS, UNITS + LAGS[-1], drain, 0)
+
     for step in range(1, 8):
         gain_copy(step).wait()
     sums = gain_own[:, 0:1]
@@ -805,13 +883,35 @@
     o_gains[...] = sums
 
     def sent(unit, carry):
-        await_arrival(got_a.at[unit], a_sends.at[unit])
-        await_arrival(got_b.at[unit], b_sends.at[unit])
-        await_arrival(got_c.at[unit], c_sends.at[unit])
+        @pl.when(added_here(unit))
+        def _():
+            await_arrival(got_a.at[unit], a_sends.at[unit])
+            await_arrival(got_b.at[unit], b_sends.at[unit])
+            await_arrival(got_c.at[unit], c_sends.at[unit])
+
         return carry
 
-    lax.fori_loop(0, UNITS, sent, 0)
-    await_arrival(total, out_sem)
+    lax.fori_loop(0, UNITS + LENT, sent, 0)
+
+    @pl.when(lender)
+    def _():
+        def returned(place, carry):
+            await_arrival(made.at[UNITS + place], lent_sends.at[place])
+            await_arrival(total.at[2 * place + 1], back_arrivals.at[place])
+            deliver(2 * place + 1)
+            return carry
+
+        lax.fori_loop(0, loan, returned, 0)
+
+    @pl.when(jnp.logical_not(lender))
+    def _():
+        def returned(place, carry):
+            await_arrival(total.at[UNITS + place], back_sends.at[place])
+            return carry
+
+        lax.fori_loop(0, loan, returned, 0)
+
+    await_arrival(total.at[pl.ds(0, UNITS)], out_sem)
 
 
 def weight_grads(na, dt, mixed, da, nm, dh, act, db, gains):
@@ -833,25 +933,30 @@
             pltpu.VMEM((2, tokens, D), BF16),
             pltpu.VMEM((2, tokens, UNIT), BF16),
             pltpu.VMEM((tokens, FF), BF16),
-            pltpu.VMEM((UNITS, 2, 2, 2, 96, UNIT), BF16),
-            pltpu.VMEM((UNITS, 2, 2, 96, UNIT), BF16),
-            pltpu.VMEM((UNITS, 2, 96, UNIT), BF16),
-            pltpu.VMEM((UNITS, 96, UNIT), BF16),
-            pltpu.VMEM((UNITS, 96, UNIT), F32),
+            pltpu.VMEM((UNITS + LENT, 2, 2, 2, 96, UNIT), BF16),
+            pltpu.VMEM((UNITS + LENT, 2, 2, 96, UNIT), BF16),
+            pltpu.VMEM((UNITS + LENT, 2, 96, UNIT), BF16),
+            pltpu.VMEM((UNITS + LENT, 96, UNIT), BF16),
+            pltpu.VMEM((UNITS + LENT, 96, UNIT), F32),
             pltpu.VMEM((2, 8, D), F32),
             pltpu.VMEM((7, 2, 8, D), F32),
             DMA((2,)),
             DMA((2,)),
             DMA,
-            DMA((UNITS,)),
-            DMA((UNITS,)),
-            DMA((UNITS,)),
-            DMA((UNITS,)),
-            DMA((UNITS,)),
-            DMA((UNITS,)),
+            DMA((UNITS + LENT,)),
+            DMA((UNITS + LENT,)),
+            DMA((UNITS + LENT,)),
+            DMA((UNITS + LENT,)),
+            DMA((UNITS + LENT,)),
+            DMA((UNITS + LENT,)),
             DMA,
             DMA((7,)),
             DMA((7,)),
+            DMA((LENT,)),
+            DMA((LENT,)),
+            DMA((LENT,)),
+            DMA((LENT,)),
+            pltpu.SemaphoreType.REGULAR,
         ],
         compiler_params=pltpu.CompilerParams(
             collective_id=2, has_side_effects=True, vmem_limit_bytes=VMEM_LIMIT
@@ -905,7 +1010,7 @@
     weights = (gain_attn, gain_mlp, w_qkv[0], w_out[0], w_up[0], w_down[0])
     output, input_grad, gains, kept = layers(sections, chunks, tokens, cotangent, doc_ids, weights)
     db, dh, da, dt = kept["db"], kept["dh"], kept["da"], kept["dt"]
-    if lax.axis_size("dp") == 8 and chunks == 8:
+    if lax.axis_size("dp") == 8 and sections == 4 and chunks == 8:
         qkv, out, up, down, gains = weight_grads(
             kept["na"], dt, kept["mixed"], da, kept["nm"], dh, kept["act"], db, gains
         )

time: 412 us -> 400 us (0.971)
  Pallas kernels: 411 us -> 399 us
    pallas_call x1, Pallas kernels: 146 us -> 135 us  [weight_grads(): pl.pallas_call(weight_grad_kernel, out_shape=[sds((96, 3 * D), F32), sds(...]
where the time goes in v5:
time: 400 us
  Pallas kernels  399 us (100%)
    pallas_call x1, Pallas kernels, layers(): pl.pallas_call(functools.partial(layer_kernel, sections), out_shape=[sds(...  259 us
    pallas_call x1, Pallas kernels, weight_grads(): pl.pallas_call(weight_grad_kernel, out_shape=[sds((96, 3 * D), F32), sds(...  135 us

profile of v5, /device:TPU:0, one launch (start us, length us, event | category | flops | bytes accessed | tf_op | source)
XLA Modules:
  0.0 399.8 jit_solution(8796477408665329084)
XLA Ops:
  0.6 258.7 %layers.1 = (bf16[2,256,768]{2,1,0:T(8,128)(2,1)}, bf16[2,256,768]{2,1,0:T(8,128)(2,1)}, f32[2,8,768]{2,1,0:T(8,128)}, bf16[8,256,768]{2,1,0:T(8,128)(2,1)}, bf1...) custom-call(bf16[2,256,768]{2,1,0:T(8,128)(2,1)} %bitcast.32, ...), custom_call_target="tpu_custom_call" | custom-call | tf_op jit(solution)/shard_map/layers/pallas_call | solution.py:526
  259.3 134.6 %weight_grads.1 = (f32[96,2304]{1,0:T(8,128)}, f32[96,768]{1,0:T(8,128)}, f32[96,3072]{1,0:T(8,128)}, f32[384,768]{1,0:T(8,128)}, f32[2,1,768]{2,1,0:T(1,128)}) custom-call(bf16[2048,768]{1,0:T(8,128)(2,1)} %bitcast.26, bf16[2048,2304]{1,0:T(8,128)(2,1)} %bitcast.22, bf16[2048,768]{1,0:T(8,128)(2,1)} %bitcast.27, bf16[2048,768]{1,0:T(8,128)(2,1)} %bitcast.30, ...), custom_call_target="tpu_custom_call" | custom-call | tf_op jit(solution)/shard_map/weight_grads/pallas_call | solution.py:921
  393.9 5.8 %hand_over.1 = (bf16[512,768]{1,0:T(8,128)(2,1)}, bf16[512,768]{1,0:T(8,128)(2,1)}, f32[96,2304]{1,0:T(8,128)}, f32[96,768]{1,0:T(8,128)}, f32[96,3072]{1,0:T(8,...) custom-call(f32[2,1,768]{2,1,0:T(1,128)} %get-tuple-element.41.gains, bf16[512,768]{1,0:T(8,128)(2,1)} %bitcast.34, ...), custom_call_target="tpu_custom_call" | custom-call | tf_op jit(solution)/shard_map/hand_over/pallas_call | solution.py:993

commit v6 on v5

--- a/solution.py
+++ b/solution.py
@@ -130,7 +130,7 @@
             await_arrival(result.at[piece], landed.at[piece])
 
 
-def fill_bias(docs, chunk, bias, keys_down):
+def fill_bias(docs, chunk, bias):
     per_row = docs.shape[1] // C
     row, place = chunk // per_row, lax.rem(chunk, per_row)
 
@@ -138,28 +138,17 @@
         start = pl.multiple_of(jnp.maximum(block, 0) * C, C)
         return docs[pl.ds(row, 1), pl.ds(start, C)].astype(F32)
 
-    def upright(line):
-        return jnp.transpose(jnp.broadcast_to(line, (128, C)))
-
     queries = numbers(place)
-    if not keys_down:
-        queries = upright(queries)
     for part in range(WIN):
-        keys = numbers(place - (WIN - 1) + part)
-        if keys_down:
-            keys = upright(keys)
+        keys = jnp.transpose(jnp.broadcast_to(numbers(place - (WIN - 1) + part), (128, C)))
         for half in range(C // 128):
             lanes = slice(half * 128, (half + 1) * 128)
-            allowed = keys == queries[:, lanes] if keys_down else queries == keys[:, lanes]
+            allowed = keys == queries[:, lanes]
             if part == WIN - 1:
                 down = lax.broadcasted_iota(jnp.int32, (C, 128), 0)
                 across = lax.broadcasted_iota(jnp.int32, (C, 128), 1) + half * 128
-                allowed = allowed & ((down <= across) if keys_down else (across <= down))
-            term = jnp.where(allowed, 0.0, NEG)
-            if keys_down:
-                bias[part * C : (part + 1) * C, lanes] = term
-            else:
-                bias[:, part * C + half * 128 : part * C + (half + 1) * 128] = term
+                allowed = allowed & (down <= across)
+            bias[part * C : (part + 1) * C, lanes] = jnp.where(allowed, 0.0, NEG)
 
 
 def by_blocks(docs, chunk, attend):
@@ -188,7 +177,7 @@
     s_q,
     s_na,
     s_mixed,
-    s_lse,
+    s_probs,
     s_mid,
     s_nm,
     s_act,
@@ -206,17 +195,16 @@
     grads,
     kbuf,
     vbuf,
-    bias_f,
-    bias_b,
+    bias,
     dk_acc,
     dv_acc,
-    lse_d,
+    inner,
     b_dmix,
     marks,
     b_q,
     b_na,
     b_mixed,
-    b_lse,
+    b_probs,
     b_mid,
     b_nm,
     b_act,
@@ -245,13 +233,14 @@
             ((h_qkv, w_qkv), (h_out, w_out), (h_up, w_up), (h_down, w_down))
         )
     ]
-    for copy in weights:
-        copy.start()
-
-    def at_first(chunk, copy):
+    weights[0].start()
+
+    def at_first(chunk, copy, *later):
         @pl.when(chunk == 0)
         def _():
             copy.wait()
+            for other in later:
+                other.start()
 
     def clear():
         dk_acc[...] = jnp.zeros_like(dk_acc)
@@ -276,7 +265,7 @@
             (b_q, s_q),
             (b_na, s_na),
             (b_mixed, s_mixed),
-            (b_lse, s_lse),
+            (b_probs, s_probs),
             (b_mid, s_mid),
             (b_nm, s_nm),
             (b_act, s_act),
@@ -296,8 +285,8 @@
                 copy.wait()
 
         todo = keep_forward(chunk, slot)
-        at_first(chunk, weights[0])
-        fill_bias(docs, chunk, bias_f, False)
+        at_first(chunk, *weights)
+        fill_bias(docs, chunk, bias)
         await_arrival(inbox.at[chunk], arrivals.at[chunk])
         x = inbox[chunk].astype(F32)
         x = x - centered * row_mean(x)
@@ -309,26 +298,29 @@
         kbuf[here, :] = dot(na, w_qkv[:, D : 2 * D]).astype(BF16)
         vbuf[here, :] = dot(na, w_qkv[:, 2 * D :]).astype(BF16)
         todo[0].start()
-        lane = lax.broadcasted_iota(jnp.int32, (1, 128), 1)
-
         def attend(blocks):
             window = pl.ds(pl.multiple_of((chunk - blocks + 1) * C, C), blocks * C)
             masked = slice((WIN - blocks) * C, WIN * C)
-            lse_all = jnp.zeros((C, 128), F32)
+            def lanes_of(pair):
+                return slice(pair * 2 * HD, (pair + 1) * 2 * HD)
+
+            def scores(pair):
+                q2 = two_heads(b_q[slot, :, lanes_of(pair)], low, high)
+                return dot_nt(kbuf[window, lanes_of(pair)], q2)
+
+            both = jnp.concatenate([bias[masked, :], bias[masked, :]], axis=1)
+            ahead = scores(0)
             for pair in range(PAIRS):
-                lanes = slice(pair * 2 * HD, (pair + 1) * 2 * HD)
-                q2 = two_heads(b_q[slot, :, lanes], low, high)
-                s = dot_nt(q2, kbuf[window, lanes]).reshape(2, C, blocks * C) + bias_f[:, masked][None]
-                top = jnp.max(s, axis=-1, keepdims=True)
-                e = jnp.exp(s - top)
-                total = jnp.sum(e, axis=-1, keepdims=True)
-                o = dot(e.astype(BF16).reshape(2 * C, blocks * C), vbuf[window, lanes])
-                o = o.reshape(2, C, 2 * HD) * (1.0 / total)
-                b_mixed[slot, :, lanes] = jnp.where(is_low, o[0], o[1]).astype(BF16)
-                lse = top + jnp.log(total)
-                lse_all = jnp.where(lane == 2 * pair, lse[0], lse_all)
-                lse_all = jnp.where(lane == 2 * pair + 1, lse[1], lse_all)
-            b_lse[slot] = jnp.transpose(lse_all)[:16]
+                s = ahead + both
+                if pair + 1 < PAIRS:
+                    ahead = scores(pair + 1)
+                e = jnp.exp(s - jnp.max(s, axis=0, keepdims=True))
+                probs = (e * (1.0 / jnp.sum(e, axis=0, keepdims=True))).astype(BF16)
+                b_probs[slot, pair, masked, :] = probs
+                o = lax.dot_general(
+                    probs, vbuf[window, lanes_of(pair)], (((0,), (0,)), ((), ())), preferred_element_type=F32
+                )
+                b_mixed[slot, :, lanes_of(pair)] = jnp.where(is_low, o[:C], o[C:]).astype(BF16)
 
         by_blocks(docs, chunk, attend)
         todo[2].start()
@@ -376,7 +368,7 @@
         clear()
 
     def fetches(chunk, slot):
-        pairs = ((s_dg, b_dg), (s_mid, b_mid), (s_mixed, b_mixed), (s_q, b_q), (s_lse, b_lse))
+        pairs = ((s_dg, b_dg), (s_mid, b_mid), (s_mixed, b_mixed), (s_q, b_q), (s_probs, b_probs))
         return [
             pltpu.make_async_copy(src.at[chunk], dst.at[slot], loads.at[kind, slot])
             for kind, (src, dst) in enumerate(pairs)
@@ -412,7 +404,6 @@
                 copy.wait()
 
         todo = keep_backward(chunk, slot)
-        fill_bias(docs, chunk, bias_b, True)
         await_arrival(grads.at[chunk], grad_arrivals.at[chunk])
         g = grads[chunk].astype(F32)
         db = (g - row_mean(g)).astype(BF16)
@@ -437,10 +428,7 @@
         dmix = dot_nt(da, w_out[...]).astype(BF16)
         b_dmix[...] = dmix
         prod = dmix.astype(F32) * b_mixed[slot].astype(F32)
-        top = prod.astype(BF16)
-        rest = (prod - top.astype(F32)).astype(BF16)
-        inner = dot(top, marks[...]) + dot(rest, marks[...])
-        lse_d[...] = jnp.transpose(inner)[:16]
+        inner[...] = jnp.transpose(dot(prod.astype(BF16), marks[...]))[:16]
         def attend(blocks):
             window = pl.ds(pl.multiple_of((chunk - blocks + 1) * C, C), blocks * C)
             masked = slice((WIN - blocks) * C, WIN * C)
@@ -449,14 +437,11 @@
                 q2 = two_heads(b_q[slot, :, lanes], low, high)
                 do2 = two_heads(b_dmix[:, lanes], low, high)
                 keys = kbuf[window, lanes]
-                values = vbuf[window, lanes]
-                both = jnp.concatenate([bias_b[masked, :], bias_b[masked, :]], axis=1)
                 even, odd = slice(2 * pair, 2 * pair + 1), slice(2 * pair + 1, 2 * pair + 2)
-                lse = jnp.concatenate([b_lse[slot, even, :], b_lse[slot, odd, :]], axis=1)
-                inner = jnp.concatenate([lse_d[even, :], lse_d[odd, :]], axis=1)
-                probs = jnp.exp(dot_nt(keys, q2) + both - lse)
-                ds = (probs * (dot_nt(values, do2) - inner)).astype(BF16)
-                dv = dot(probs.astype(BF16), do2)
+                mean = jnp.concatenate([inner[even, :], inner[odd, :]], axis=1)
+                probs = b_probs[slot, pair, masked, :]
+                ds = (probs.astype(F32) * (dot_nt(vbuf[window, lanes], do2) - mean)).astype(BF16)
+                dv = dot(probs, do2)
                 dk = dot(ds, q2)
                 for part in range(blocks):
                     place = lax.rem(chunk - blocks + 1 + part, WIN)
@@ -511,7 +496,7 @@
         ("q", (C, D), BF16),
         ("na", (C, D), BF16),
         ("mixed", (C, D), BF16),
-        ("lse", (16, C), F32),
+        ("probs", (PAIRS, WIN * C, 2 * C), BF16),
         ("mid", (C, D), F32),
         ("nm", (C, D), BF16),
         ("act", (C, FF), BF16),
@@ -537,7 +522,6 @@
             pltpu.VMEM((chunks, C, D), BF16),
             pltpu.VMEM((chunks * C, D), BF16),
             pltpu.VMEM((chunks * C, D), BF16),
-            pltpu.VMEM((C, WIN * C), F32),
             pltpu.VMEM((WIN * C, C), F32),
             pltpu.VMEM((WIN, C, D), F32),
             pltpu.VMEM((WIN, C, D), F32),
@@ -662,8 +646,6 @@
 
     load_left(s_na, 0).start()
     start_right(0)
-    load_left(s_mixed, 1).start()
-    pltpu.make_async_copy(s_act, act, act_sem).start()
     gain_own[...] = jnp.sum(gains[...], axis=1, keepdims=True) + jnp.zeros((2, 8, D), F32)
 
     barrier = pltpu.get_barrier_semaphore()
@@ -793,6 +775,11 @@
     def narrow(unit, carry):
         slot = lax.rem(unit, 2)
         side = jnp.where((unit >= 9) & (unit < 12), 1, 0)
+
+        @pl.when(unit == 1)
+        def _():
+            load_left(s_mixed, 1).start()
+            pltpu.make_async_copy(s_act, act, act_sem).start()
 
         @pl.when(unit == 9)
         def _():

time: 400 us -> 396 us (0.990)
  Pallas kernels: 399 us -> 394 us
    pallas_call x1, Pallas kernels: 259 us -> 253 us  [layers(): pl.pallas_call(functools.partial(layer_kernel, sections), out_shape=[sds(...]
where the time goes in v6:
time: 396 us; the launch traced here: 394 us
  Pallas kernels  394 us (99%)
    pallas_call x1, Pallas kernels, layers(): pl.pallas_call(functools.partial(layer_kernel, sections), out_shape=[sds(...  253 us
    pallas_call x1, Pallas kernels, weight_grads(): pl.pallas_call(weight_grad_kernel, out_shape=[sds((96, 3 * D), F32), sds(...  135 us

profile of v6, /device:TPU:0, one launch (start us, length us, event | category | flops | bytes accessed | tf_op | source)
XLA Modules:
  0.0 394.4 jit_solution(8034075568824308727)
XLA Ops:
  0.6 253.0 %layers.1 = (bf16[2,256,768]{2,1,0:T(8,128)(2,1)}, bf16[2,256,768]{2,1,0:T(8,128)(2,1)}, f32[2,8,768]{2,1,0:T(8,128)}, bf16[8,256,768]{2,1,0:T(8,128)(2,1)}, bf1...) custom-call(bf16[2,256,768]{2,1,0:T(8,128)(2,1)} %bitcast.32, ...), custom_call_target="tpu_custom_call" | custom-call | tf_op jit(solution)/shard_map/layers/pallas_call | solution.py:511
  253.7 134.8 %weight_grads.1 = (f32[96,2304]{1,0:T(8,128)}, f32[96,768]{1,0:T(8,128)}, f32[96,3072]{1,0:T(8,128)}, f32[384,768]{1,0:T(8,128)}, f32[2,1,768]{2,1,0:T(1,128)}) custom-call(bf16[2048,768]{1,0:T(8,128)(2,1)} %bitcast.26, bf16[2048,2304]{1,0:T(8,128)(2,1)} %bitcast.22, bf16[2048,768]{1,0:T(8,128)(2,1)} %bitcast.27, bf16[2048,768]{1,0:T(8,128)(2,1)} %bitcast.30, ...), custom_call_target="tpu_custom_call" | custom-call | tf_op jit(solution)/shard_map/weight_grads/pallas_call | solution.py:908
  388.5 5.8 %hand_over.1 = (bf16[512,768]{1,0:T(8,128)(2,1)}, bf16[512,768]{1,0:T(8,128)(2,1)}, f32[96,2304]{1,0:T(8,128)}, f32[96,768]{1,0:T(8,128)}, f32[96,3072]{1,0:T(8,...) custom-call(f32[2,1,768]{2,1,0:T(1,128)} %get-tuple-element.41.gains, bf16[512,768]{1,0:T(8,128)(2,1)} %bitcast.34, ...), custom_call_target="tpu_custom_call" | custom-call | tf_op jit(solution)/shard_map/hand_over/pallas_call | solution.py:980

commit v7 on v6

--- a/solution.py
+++ b/solution.py
@@ -646,7 +646,7 @@
 
     load_left(s_na, 0).start()
     start_right(0)
-    gain_own[...] = jnp.sum(gains[...], axis=1, keepdims=True) + jnp.zeros((2, 8, D), F32)
+    gain_own[...] = jnp.sum(gains[...], axis=1)
 
     barrier = pltpu.get_barrier_semaphore()
     for step in range(1, 8):
@@ -864,10 +864,10 @@
 
     for step in range(1, 8):
         gain_copy(step).wait()
-    sums = gain_own[:, 0:1]
+    sums = gain_own[...]
     for step in range(7):
-        sums = sums + gain_in[step, :, 0:1]
-    o_gains[...] = sums
+        sums = sums + gain_in[step]
+    o_gains[...] = sums[:, None, :]
 
     def sent(unit, carry):
         @pl.when(added_here(unit))
@@ -925,8 +925,8 @@
             pltpu.VMEM((UNITS + LENT, 2, 96, UNIT), BF16),
             pltpu.VMEM((UNITS + LENT, 96, UNIT), BF16),
             pltpu.VMEM((UNITS + LENT, 96, UNIT), F32),
-            pltpu.VMEM((2, 8, D), F32),
-            pltpu.VMEM((7, 2, 8, D), F32),
+            pltpu.VMEM((2, D), F32),
+            pltpu.VMEM((7, 2, D), F32),
             DMA((2,)),
             DMA((2,)),
             DMA,

time: 396 us -> 394 us (level)
  no operation moved by 1% of the time
where the time goes in v7:
time: 394 us; the launch traced here: 392 us
  Pallas kernels  391 us (99%)
    pallas_call x1, Pallas kernels, layers(): pl.pallas_call(functools.partial(layer_kernel, sections), out_shape=[sds(...  253 us
    pallas_call x1, Pallas kernels, weight_grads(): pl.pallas_call(weight_grad_kernel, out_shape=[sds((96, 3 * D), F32), sds(...  132 us

profile of v7, /device:TPU:0, one launch (start us, length us, event | category | flops | bytes accessed | tf_op | source)
XLA Modules:
  0.0 392.1 jit_solution(4787348867722575204)
XLA Ops:
  0.6 253.0 %layers.1 = (bf16[2,256,768]{2,1,0:T(8,128)(2,1)}, bf16[2,256,768]{2,1,0:T(8,128)(2,1)}, f32[2,8,768]{2,1,0:T(8,128)}, bf16[8,256,768]{2,1,0:T(8,128)(2,1)}, bf1...) custom-call(bf16[2,256,768]{2,1,0:T(8,128)(2,1)} %bitcast.32, ...), custom_call_target="tpu_custom_call" | custom-call | tf_op jit(solution)/shard_map/layers/pallas_call | solution.py:511
  253.7 132.5 %weight_grads.1 = (f32[96,2304]{1,0:T(8,128)}, f32[96,768]{1,0:T(8,128)}, f32[96,3072]{1,0:T(8,128)}, f32[384,768]{1,0:T(8,128)}, f32[2,1,768]{2,1,0:T(1,128)}) custom-call(bf16[2048,768]{1,0:T(8,128)(2,1)} %bitcast.26, bf16[2048,2304]{1,0:T(8,128)(2,1)} %bitcast.22, bf16[2048,768]{1,0:T(8,128)(2,1)} %bitcast.27, bf16[2048,768]{1,0:T(8,128)(2,1)} %bitcast.30, ...), custom_call_target="tpu_custom_call" | custom-call | tf_op jit(solution)/shard_map/weight_grads/pallas_call | solution.py:908
  386.1 5.8 %hand_over.1 = (bf16[512,768]{1,0:T(8,128)(2,1)}, bf16[512,768]{1,0:T(8,128)(2,1)}, f32[96,2304]{1,0:T(8,128)}, f32[96,768]{1,0:T(8,128)}, f32[96,3072]{1,0:T(8,...) custom-call(f32[2,1,768]{2,1,0:T(1,128)} %get-tuple-element.41.gains, bf16[512,768]{1,0:T(8,128)(2,1)} %bitcast.34, ...), custom_call_target="tpu_custom_call" | custom-call | tf_op jit(solution)/shard_map/hand_over/pallas_call | solution.py:980
